TPU v7x, 128 devices: a whole 4x4x4 slice. The times are simulated.
128 devices in a mesh: col: 32 (over x, y, core), row: 4 (over z).
Axes of the slice: x: 4, y: 4, z: 4, core: 2. Of those that a mesh axis runs over, the one named last changes fastest.
Arguments:
- rhs: float32 [2, 32, 4, 4096], P(None, None, 'row', 'col'), may hold values from -6 to 6
- u_factor: bfloat16 [64, 160, 2, 256, 128], P('row', 'col'), may hold values from -0.0390625 to 0.0390625
- v_factor: bfloat16 [64, 160, 2, 256, 128], P('row', 'col'), may hold values from -0.375 to 0.375
- ranks: int32 [64, 160], P('row', 'col'), may hold values from 8 to 128, as said below
- assign: int32 [160], replicated, may hold values from 0 to 159, each once
Outputs:
- solution: float32 [2, 32, 40960], P(None, None, 'col')
- residual_estimate: float32 [32], replicated
Inputs may be any that keep to these rules, and one draw needn't show every extreme that they name: `ranks`: every entry is 128 // 16 times a power of two from 1 to 16.
All inputs are finite; a program needn't handle non-finite values.
Results may differ from a plain program's by a relative error of at most 0.0068.
Values may be sent and summed in bfloat16 or wider, within the bound.
A program may use at most 128 MiB of HBM per device.

v0:
```python
import jax
import jax.numpy as jnp
from jax import lax
from jax.sharding import Mesh
from jax.sharding import PartitionSpec as P

ITERS = 2
COL = ("col_0", "col_1", "col_2")
COL_ROW = ("col_0", "col_1", "col_2", "row")


def cut_along(x, dim, devices):
    before, after = (x.shape[:dim], x.shape[dim + 1 :])
    return jnp.moveaxis(x.reshape(*before, devices, -1, *after), dim, 0)


def sent_and_summed(x, axis, dim):
    devices = lax.axis_size(axis)
    tiles = lax.all_to_all(cut_along(x, dim, devices), axis, 0, 0, tiled=True)
    return jnp.sum(tiles.astype(jnp.float32), axis=0)


def in_order(tiles, dim):
    tiles = jnp.moveaxis(tiles, 0, dim)
    dims = tiles.shape
    return tiles.reshape(*dims[:dim], dims[dim] * dims[dim + 1], *dims[dim + 2 :])


def copy_for_each(x, axis):
    copies = jnp.broadcast_to(x, (lax.axis_size(axis), *x.shape))
    return lax.all_to_all(copies, axis, split_axis=0, concat_axis=0, tiled=True)


def collect(x, axis, dim):
    return in_order(copy_for_each(x, axis), dim)


def by_axis(x, axes):
    for axis in axes:
        x = lax.psum(x, axis)
    return x


def over_copies(x, axis):
    everything = copy_for_each(x, axis)
    return jnp.sum(everything.astype(jnp.float32), axis=0)


def over_copies_2(x, axis):
    everything = copy_for_each(x, axis)
    return jnp.sum(everything, axis=0)


def sum_squares(value):
    return jnp.sum(value * value, axis=(0, 2))


def on_device(rhs, u_factor, v_factor, ranks, assign):
    tile_rows = u_factor.shape[0]
    tile_cols = u_factor.shape[1]
    tile_size = u_factor.shape[3]
    rank_cap = u_factor.shape[4]
    sources = rhs.shape[1]
    rank_iota = lax.broadcasted_iota(jnp.int32, (tile_rows, tile_cols, 1, 1, rank_cap), 4)
    mask = (rank_iota < ranks[:, :, None, None, None]).astype(jnp.float32)

    def adjoint_terms(group_data):
        data_b = group_data.reshape(2, sources, tile_rows, tile_size)
        raw = jnp.einsum("ipcnk,dsin->ipcdsk", u_factor, data_b, preferred_element_type=jnp.float32)
        coeff = jnp.stack(
            [raw[:, :, 0, 0] + raw[:, :, 1, 1], raw[:, :, 0, 1] - raw[:, :, 1, 0]], axis=2
        )
        coeff = (coeff * mask).astype(jnp.bfloat16)
        prod = jnp.einsum("ipcnk,ipdsk->cdspn", v_factor, coeff, preferred_element_type=jnp.float32)
        partial_model = jnp.stack([prod[0, 0] + prod[1, 1], prod[0, 1] - prod[1, 0]], axis=0)
        return partial_model.reshape(2, sources, tile_cols * tile_size)

    def adjoint_step(data_hat, v_prev):
        group_data = collect(data_hat.astype(jnp.bfloat16), COL, 2)
        beta_now = jnp.sqrt(by_axis(sum_squares(data_hat), COL_ROW))
        model_sum = over_copies(adjoint_terms(group_data).astype(jnp.bfloat16), "row").astype(
            jnp.float32
        )
        v_hat = model_sum / beta_now[None, :, None] - beta_now[None, :, None] * v_prev
        alpha_now = jnp.sqrt(over_copies_2(sum_squares(v_hat), COL))
        return (
            data_hat / beta_now[None, :, None],
            beta_now,
            v_hat / alpha_now[None, :, None],
            alpha_now,
        )

    data_first = rhs.reshape(2, sources, rhs.shape[3])
    zero_model = jnp.zeros((2, sources, tile_cols * tile_size), jnp.float32)
    u_vec, beta_now, v_vec, alpha_now = adjoint_step(data_first, zero_model)
    w_vec = v_vec
    x_vec = zero_model
    phibar = beta_now
    rhobar = alpha_now
    for iteration in range(ITERS):
        model_b = v_vec.astype(jnp.bfloat16).reshape(2, sources, tile_cols, tile_size)
        forward_raw = jnp.einsum(
            "ipcnk,dspn->ipcdsk", v_factor, model_b, preferred_element_type=jnp.float32
        )
        forward_coeff = jnp.stack(
            [
                forward_raw[:, :, 0, 0] - forward_raw[:, :, 1, 1],
                forward_raw[:, :, 0, 1] + forward_raw[:, :, 1, 0],
            ],
            axis=2,
        )
        forward_coeff = (forward_coeff * mask).astype(jnp.bfloat16)
        forward_prod = jnp.einsum(
            "ipcnk,ipdsk->cdsin", u_factor, forward_coeff, preferred_element_type=jnp.float32
        )
        partial_data = jnp.stack(
            [forward_prod[0, 0] - forward_prod[1, 1], forward_prod[0, 1] + forward_prod[1, 0]],
            axis=0,
        )
        partial_data = partial_data.reshape(2, sources, tile_rows * tile_size)
        data_hat = (
            sent_and_summed(partial_data.astype(jnp.bfloat16), COL, 2)
            - alpha_now[None, :, None] * u_vec
        )
        u_vec, beta_now, v_vec, alpha_now = adjoint_step(data_hat, v_vec)
        rho_now = jnp.sqrt(rhobar * rhobar + beta_now * beta_now)
        cosine = rhobar / rho_now
        sine = beta_now / rho_now
        theta = sine * alpha_now
        rhobar = -cosine * alpha_now
        phi_now = cosine * phibar
        phibar = sine * phibar
        x_vec = x_vec + (phi_now / rho_now)[None, :, None] * w_vec
        w_vec = v_vec - (theta / rho_now)[None, :, None] * w_vec
    all_cols = assign.shape[0]
    natural = lax.axis_index(COL) * tile_cols + jnp.arange(tile_cols, dtype=jnp.int32)
    positions = jnp.arange(all_cols, dtype=jnp.int32)
    where_held = jnp.sum(
        positions[None, :] * (assign[None, :] == natural[:, None]).astype(jnp.int32), axis=1
    )
    share = sources // lax.axis_size("row")
    own_share = lax.dynamic_slice_in_dim(x_vec, lax.axis_index("row") * share, share, 1)
    gathered = collect(own_share, COL, 2)
    gathered = gathered.reshape(2, share, all_cols, tile_size)
    picked = jnp.take(gathered, where_held, axis=2).reshape(2, share, tile_cols * tile_size)
    solution = collect(picked, "row", 1)
    return (solution, phibar)


def solution(mesh):
    split = Mesh(
        mesh.devices.reshape(4, 4, 2, mesh.shape["row"]), ("col_0", "col_1", "col_2", "row")
    )
    placed = (
        P(None, None, "row", COL),
        P("row", COL, None, None, None),
        P("row", COL, None, None, None),
        P("row", COL),
        P(),
    )
    return jax.shard_map(
        on_device, mesh=split, in_specs=placed, out_specs=(P(None, None, COL), P()), check_vma=False
    )
```

profile of v0, /device:TPU:0, one launch (start us, length us, event | category | flops | bytes accessed | tf_op | source)
XLA Modules:
  0.0 301.4 jit_solution(13848021169827376200)
XLA Ops:
  0.6 0.8 convert_element_type.53
  1.4 0.9 broadcast_in_dim.61
  2.3 7.4 %all-to-all-start = ((bf16[32,2,32,128]{3,2,1,0:T(8,128)(2,1)}), bf16[32,2,32,128]{3,2,1,0:T(8,128)(2,1)S(1)}, u32[]{:S(2)}, u32[]{:S(2)}) async-start(bf16[32,2,32,128]{3,2,1,0:T(8,128)(2,1)} %broadcast_in_dim.61), calls=%async_computation | async-start | bytes 1048576 | tf_op jit(solution)/shard_map/all_to_all | solution.py:31
  9.7 0.8 copy.231
  10.6 10.3 %all-to-all-done = bf16[32,2,32,128]{3,2,1,0:T(8,128)(2,1)S(1)} async-done(((bf16[32,2,32,128]{3,2,1,0:T(8,128)(2,1)}), bf16[32,2,32,128]{3,2,1,0:T(8,128)(2,1)S(1)}, u32[]{:S(2)}, u32[]{:S(2)}) %all-to-all-start) | async-done | bytes 524320 | tf_op jit(solution)/shard_map/all_to_all | solution.py:31
  20.9 0.3 copy.227
  21.3 0.2 reshape_reshape.9
  21.5 6.0 %fusion.29 = f32[16,5,2,2,32,128]{5,4,2,1,3,0:T(8,128)S(1)} fusion(bf16[16,5,2,256,128]{4,3,2,1,0:T(8,128)(2,1)} %param.6, bf16[2,32,16,256,1,1]{3,2,1,0,5,4:T(8,128)(2,1)S(1)} %bitcast.189), kind=kOutput, calls=%fused_computation.28 | convolution fusion | flops 671088640 | bytes 16252928 | tf_op jit(solution)/shard_map/ipcnk,dsin->ipcdsk/dot_general | solution.py:69
  27.4 0.3 fusion.48
  27.7 0.3 fusion.50
  28.0 0.3 slice-done.8
  28.3 3.3 %fusion.55 = f32[2,2,32,5,256]{4,2,0,1,3:T(8,128)S(1)} fusion(bf16[16,5,2,256,128]{4,3,2,1,0:T(8,128)(2,1)S(1)} %bitcast.181, f32[16,5,1,32,128]{4,3,1,0,2:T(8,128)S(1)} %fusion.48, f32[16,5,1,32,128]{4,3,1,0,2:T(8,128)S(1)} %fusion.50, f32[16,5,128]{2,1,0:T(8,128)S(1)} %fusion.88), kind=kOutput, calls=%fused_computation.59 | convolution fusion | flops 673054720 | bytes 13803520 | tf_op jit(solution)/shard_map/ipcnk,ipdsk->cdspn/dot_general | solution.py:74
  32.0 0.9 broadcast_in_dim.62
  32.9 5.3 %all-to-all-start.1 = ((bf16[4,2,32,1280]{3,2,1,0:T(8,128)(2,1)}), bf16[4,2,32,1280]{3,2,1,0:T(8,128)(2,1)S(1)}, u32[]{:S(2)}, u32[]{:S(2)}) async-start(bf16[4,2,32,1280]{3,2,1,0:T(8,128)(2,1)} %broadcast_in_dim.62), calls=%async_computation.1 | async-start | bytes 1310720 | tf_op jit(solution)/shard_map/all_to_all | solution.py:31
  38.3 8.9 %psum.84 = f32[32]{0:T(128)S(1)} all-reduce(f32[32]{0:T(128)S(1)} %multiply_reduce_fusion.4), channel_id=1, replica_groups=mesh['col_0'=4,'col_1'=4,'col_2'=2,'row'=4] {'col_0'}, use_global_device_ids=true, to_apply=%region_3.0 | all-reduce | flops 32 | bytes 256 | tf_op jit(solution)/shard_map/psum | solution.py:40
  47.2 9.2 %psum.85 = f32[32]{0:T(128)S(1)} all-reduce(f32[32]{0:T(128)S(1)} %psum.84), channel_id=1, replica_groups=mesh['col_0'=4,'col_1'=4,'col_2'=2,'row'=4] {'col_1'}, use_global_device_ids=true, to_apply=%region_4.0 | all-reduce | flops 32 | bytes 256 | tf_op jit(solution)/shard_map/psum | solution.py:40
  56.4 2.4 psum.86
  58.9 10.9 %psum.87 = f32[32]{0:T(128)S(1)} all-reduce(f32[32]{0:T(128)S(1)} %psum.86), channel_id=1, replica_groups=mesh['col_0'=4,'col_1'=4,'col_2'=2,'row'=4] {'row'}, use_global_device_ids=true, to_apply=%region_6.0 | all-reduce | flops 32 | bytes 256 | tf_op jit(solution)/shard_map/psum | solution.py:40
  69.9 0.2 multiply_reduce_fusion.1
  70.2 10.5 %all_to_all.52 = f32[32,1,32]{2,1,0:T(1,128)S(1)} all-to-all(f32[32,1,32]{2,1,0:T(1,128)S(1)} %broadcast_in_dim.64), channel_id=1, replica_groups=mesh['col_0'=4,'col_1'=4,'col_2'=2,'row'=4] {'col_0','col_1','col_2'}, dimensions={0} | all-to-all | bytes 8192 | tf_op jit(solution)/shard_map/all_to_all | solution.py:31
  80.7 5.3 %fusion.20 = f32[16,5,2,2,32,128]{5,4,1,0,3,2:T(8,128)S(1)} fusion(f32[2,4,5,8,256]{4,3,2,1,0:T(8,128)S(1)} %bitcast.185, f32[32]{0:T(128)S(1)} %sqrt.30, f32[32]{0:T(128)S(1)} %get-tuple-element.29, f32[32]{0:T(128)S(1)} %get-tuple-element.28, bf16[16,5,2,256,128]{4,3,2,1,0:T(8,128)(2,1)} %param.7), kind=kOutput, calls=%fused_computation.25 | convolution fusion | flops 671416320 | bytes 16056704 | tf_op jit(solution)/shard_map/ipcnk,dspn->ipcdsk/dot_general | solution.py:102
  86.0 1.7 fusion.47
  87.7 4.6 %fusion.32 = f32[2,2,32,16,256]{4,2,0,1,3:T(8,128)S(1)} fusion(bf16[16,5,2,256,128]{4,3,2,1,0:T(8,128)(2,1)S(1)} %bitcast.177, f32[16,5,1,32,128]{4,3,1,0,2:T(8,128)} %get-tuple-element.16, f32[16,5,1,32,128]{4,3,1,0,2:T(8,128)S(1)} %get-tuple-element.15, f32[16,5,128]{2,1,0:T(8,128)S(1)} %fusion.88), kind=kOutput, calls=%fused_computation.29 | convolution fusion | flops 673054720 | bytes 15245312 | tf_op jit(solution)/shard_map/ipcnk,ipdsk->cdsin/dot_general | solution.py:113
  93.1 0.2 copy.245
  93.3 14.5 %all_to_all.53 = bf16[32,2,32,128]{3,2,1,0:T(8,128)(2,1)S(1)} all-to-all(bf16[32,2,32,128]{3,2,1,0:T(8,128)(2,1)S(1)} %copy.245), channel_id=1, replica_groups=mesh['col_0'=4,'col_1'=4,'col_2'=2,'row'=4] {'col_0','col_1','col_2'}, dimensions={0} | all-to-all | bytes 1048576 | tf_op jit(solution)/shard_map/all_to_all | solution.py:19
  107.9 0.2 multiply_reduce_fusion.3
  108.2 15.0 %all_to_all.54 = bf16[32,2,32,128]{3,2,1,0:T(8,128)(2,1)S(1)} all-to-all(bf16[32,2,32,128]{3,2,1,0:T(8,128)(2,1)S(1)} %broadcast_in_dim.65), channel_id=1, replica_groups=mesh['col_0'=4,'col_1'=4,'col_2'=2,'row'=4] {'col_0','col_1','col_2'}, dimensions={0} | all-to-all | bytes 1048576 | tf_op jit(solution)/shard_map/all_to_all | solution.py:31
  123.2 0.3 copy.246
  123.8 5.3 %fusion.26 = f32[16,5,2,2,32,128]{5,4,1,0,3,2:T(8,128)S(1)} fusion(bf16[2,32,16,256,1,1]{3,2,1,0,5,4:T(8,128)(2,1)S(1)} %bitcast.187, bf16[16,5,2,256,128]{4,3,2,1,0:T(8,128)(2,1)} %param.6), kind=kOutput, calls=%fused_computation.27 | convolution fusion | flops 671088640 | bytes 16252928 | tf_op jit(solution)/shard_map/ipcnk,dsin->ipcdsk/dot_general | solution.py:69
  129.1 0.6 fusion.45
  129.8 0.7 slice-done.11
  130.5 3.3 %fusion.60 = f32[2,2,32,5,256]{4,2,0,1,3:T(8,128)S(1)} fusion(bf16[16,5,2,256,128]{4,3,2,1,0:T(8,128)(2,1)S(1)} %bitcast.183, f32[16,5,1,32,128]{4,3,1,0,2:T(8,128)S(1)} %get-tuple-element.14, f32[16,5,1,32,128]{4,3,1,0,2:T(8,128)S(1)} %get-tuple-element.13, f32[16,5,128]{2,1,0:T(8,128)S(1)} %copy-done.2), kind=kOutput, calls=%fused_computation.60 | convolution fusion | flops 673054720 | bytes 13803520 | tf_op jit(solution)/shard_map/ipcnk,ipdsk->cdspn/dot_general | solution.py:74
  134.1 0.9 broadcast_in_dim.66
  135.0 3.5 %all-to-all-start.5 = ((bf16[4,2,32,1280]{3,2,1,0:T(8,128)(2,1)}), bf16[4,2,32,1280]{3,2,1,0:T(8,128)(2,1)S(1)}, u32[]{:S(2)}, u32[]{:S(2)}) async-start(bf16[4,2,32,1280]{3,2,1,0:T(8,128)(2,1)} %broadcast_in_dim.66), calls=%async_computation.5 | async-start | bytes 1310720 | tf_op jit(solution)/shard_map/all_to_all | solution.py:31
  138.5 8.9 %psum.88 = f32[32]{0:T(128)S(1)} all-reduce(f32[32]{0:T(128)S(1)} %get-tuple-element.9), channel_id=1, replica_groups=mesh['col_0'=4,'col_1'=4,'col_2'=2,'row'=4] {'col_0'}, use_global_device_ids=true, to_apply=%region_11.0 | all-reduce | flops 32 | bytes 256 | tf_op jit(solution)/shard_map/psum | solution.py:40
  147.4 9.2 %psum.89 = f32[32]{0:T(128)S(1)} all-reduce(f32[32]{0:T(128)S(1)} %psum.88), channel_id=1, replica_groups=mesh['col_0'=4,'col_1'=4,'col_2'=2,'row'=4] {'col_1'}, use_global_device_ids=true, to_apply=%region_12.0 | all-reduce | flops 32 | bytes 256 | tf_op jit(solution)/shard_map/psum | solution.py:40
  156.6 2.4 psum.90
  159.1 10.9 %psum.91 = f32[32]{0:T(128)S(1)} all-reduce(f32[32]{0:T(128)S(1)} %psum.90), channel_id=1, replica_groups=mesh['col_0'=4,'col_1'=4,'col_2'=2,'row'=4] {'row'}, use_global_device_ids=true, to_apply=%region_14.0 | all-reduce | flops 32 | bytes 256 | tf_op jit(solution)/shard_map/psum | solution.py:40
  170.1 1.1 multiply_reduce_fusion
  171.2 10.3 %all_to_all.55 = f32[32,1,32]{2,1,0:T(1,128)S(1)} all-to-all(f32[32,1,32]{2,1,0:T(1,128)S(1)} %broadcast_in_dim.67), channel_id=1, replica_groups=mesh['col_0'=4,'col_1'=4,'col_2'=2,'row'=4] {'col_0','col_1','col_2'}, dimensions={0} | all-to-all | bytes 8192 | tf_op jit(solution)/shard_map/all_to_all | solution.py:31
  181.6 5.3 %fusion.23 = f32[16,5,2,2,32,128]{5,4,1,0,3,2:T(8,128)S(1)} fusion(f32[2,4,5,8,256]{4,3,2,1,0:T(8,128)S(1)} %bitcast.188, f32[32]{0:T(128)S(1)} %sqrt.33, f32[32]{0:T(128)S(1)} %sqrt.31, f32[2,4,5,8,256]{4,3,2,1,0:T(8,128)S(1)} %bitcast.186, f32[32]{0:T(128)S(1)} %sqrt.30, f32[32]{0:T(128)S(1)} %get-tuple-element.29, f32[32]{0:T(128)S(1)} %get-tuple-element.28, ...), kind=kOutput, calls=%fused_computation.26 | convolution fusion | flops 671744000 | bytes 16384640 | tf_op jit(solution)/shard_map/ipcnk,dspn->ipcdsk/dot_general | solution.py:102
  186.9 0.6 fusion.43
  187.6 0.5 slice-done.5
  188.1 3.5 %fusion.35 = f32[2,2,32,16,256]{4,2,0,1,3:T(8,128)S(1)} fusion(bf16[16,5,2,256,128]{4,3,2,1,0:T(8,128)(2,1)S(1)} %bitcast.179, f32[16,5,1,32,128]{4,3,1,0,2:T(8,128)S(1)} %get-tuple-element.12, f32[16,5,1,32,128]{4,3,1,0,2:T(8,128)S(1)} %get-tuple-element.11, f32[16,5,128]{2,1,0:T(8,128)S(1)} %copy-done.2), kind=kOutput, calls=%fused_computation.30 | convolution fusion | flops 673054720 | bytes 15245312 | tf_op jit(solution)/shard_map/ipcnk,ipdsk->cdsin/dot_general | solution.py:113
  192.3 1.0 copy.262
  193.3 3.9 %all-to-all-start.7 = ((bf16[32,2,32,128]{3,2,1,0:T(8,128)(2,1)}), bf16[32,2,32,128]{3,2,1,0:T(8,128)(2,1)S(1)}, u32[]{:S(2)}, u32[]{:S(2)}) async-start(bf16[32,2,32,128]{3,2,1,0:T(8,128)(2,1)} %copy.262), calls=%async_computation.7 | async-start | bytes 1048576 | tf_op jit(solution)/shard_map/all_to_all | solution.py:19
  197.3 11.1 %all-to-all-done.7 = bf16[32,2,32,128]{3,2,1,0:T(8,128)(2,1)S(1)} async-done(((bf16[32,2,32,128]{3,2,1,0:T(8,128)(2,1)}), bf16[32,2,32,128]{3,2,1,0:T(8,128)(2,1)S(1)}, u32[]{:S(2)}, u32[]{:S(2)}) %all-to-all-start.7) | async-done | bytes 524320 | tf_op jit(solution)/shard_map/all_to_all | solution.py:19
  208.5 0.2 multiply_reduce_fusion.2
  208.6 8.9 %psum.92 = f32[32]{0:T(128)S(1)} all-reduce(f32[32]{0:T(128)S(1)} %multiply_reduce_fusion.2), channel_id=1, replica_groups=mesh['col_0'=4,'col_1'=4,'col_2'=2,'row'=4] {'col_0'}, use_global_device_ids=true, to_apply=%region_20.0 | all-reduce | flops 32 | bytes 256 | tf_op jit(solution)/shard_map/psum | solution.py:40
  217.6 9.2 %psum.93 = f32[32]{0:T(128)S(1)} all-reduce(f32[32]{0:T(128)S(1)} %psum.92), channel_id=1, replica_groups=mesh['col_0'=4,'col_1'=4,'col_2'=2,'row'=4] {'col_1'}, use_global_device_ids=true, to_apply=%region_21.0 | all-reduce | flops 32 | bytes 256 | tf_op jit(solution)/shard_map/psum | solution.py:40
  226.7 2.4 psum.94
  229.2 7.7 %psum.95 = f32[32]{0:T(128)S(1)} all-reduce(f32[32]{0:T(128)S(1)} %psum.94), channel_id=1, replica_groups=mesh['col_0'=4,'col_1'=4,'col_2'=2,'row'=4] {'row'}, use_global_device_ids=true, to_apply=%region_23.0 | all-reduce | flops 32 | bytes 256 | tf_op jit(solution)/shard_map/psum | solution.py:40
  236.9 0.6 divide_multiply_fusion
  237.7 1.0 fusion.87
  238.7 1.8 broadcast_in_dim.68
  240.5 4.4 %all-to-all-start.8 = ((f32[32,2,8,1280]{3,2,1,0:T(8,128)}), f32[32,2,8,1280]{3,2,1,0:T(8,128)S(1)}, u32[]{:S(2)}, u32[]{:S(2)}) async-start(f32[32,2,8,1280]{3,2,1,0:T(8,128)} %broadcast_in_dim.68), calls=%async_computation.8 | async-start | bytes 5242880 | tf_op jit(solution)/shard_map/all_to_all | solution.py:31
  245.0 0.2 select_reduce_fusion
  245.3 34.1 %all-to-all-done.8 = f32[32,2,8,1280]{3,2,1,0:T(8,128)S(1)} async-done(((f32[32,2,8,1280]{3,2,1,0:T(8,128)}), f32[32,2,8,1280]{3,2,1,0:T(8,128)S(1)}, u32[]{:S(2)}, u32[]{:S(2)}) %all-to-all-start.8) | async-done | bytes 2621472 | tf_op jit(solution)/shard_map/all_to_all | solution.py:31
  279.4 3.0 %copy.263 = f32[2,8,32,1280]{3,2,1,0:T(8,128)} copy(f32[2,8,32,1280]{3,1,0,2:T(8,128)S(1)} %bitcast.184) | data formatting | bytes 5242880 | tf_op jit(solution)/shard_map/transpose | solution.py:24
  282.4 2.7 reshape_reshape.11
  285.1 3.0 %copy.264 = f32[2,8,160,256]{3,1,2,0:T(8,128)} copy(f32[2,8,160,256]{3,2,1,0:T(8,128)S(1)} %reshape_reshape.11) | data formatting | bytes 5242880 | tf_op jit(solution)/shard_map/reshape;reshape | solution.py:144
  288.1 2.3 gather_fusion
  290.5 10.1 %all_to_all.56 = f32[4,2,8,1280]{3,2,1,0:T(8,128)S(1)} all-to-all(f32[4,2,8,1280]{3,2,1,0:T(8,128)S(1)} %broadcast_in_dim.70), channel_id=1, replica_groups=mesh['col_0'=4,'col_1'=4,'col_2'=2,'row'=4] {'row'}, dimensions={0} | all-to-all | bytes 655360 | tf_op jit(solution)/shard_map/all_to_all | solution.py:31
  300.6 0.7 copy.380
  (90 shorter events, 3.7 us)
Async XLA Ops:
  2.3 18.6 %all-to-all-start = ((bf16[32,2,32,128]{3,2,1,0:T(8,128)(2,1)}), bf16[32,2,32,128]{3,2,1,0:T(8,128)(2,1)S(1)}, u32[]{:S(2)}, u32[]{:S(2)}) async-start(bf16[32,2,32,128]{3,2,1,0:T(8,128)(2,1)} %broadcast_in_dim.61), calls=%async_computation | async-start | bytes 1048576 | tf_op jit(solution)/shard_map/all_to_all | solution.py:31
  10.6 77.2 %copy-start.1 = (f32[16,5,128]{2,1,0:T(8,128)}, f32[16,5,128]{2,1,0:T(8,128)S(1)}, u32[]{:S(2)}) copy-start(f32[16,5,128]{2,1,0:T(8,128)S(1)} %fusion.88) | copy-start | bytes 122884
  21.2 6.8 %slice-start.6 = ((s8[10485760]{0:T(1024)(128)(4,1)}), s8[2097152]{0:T(1024)(128)(4,1)S(1)}, s32[]{:S(2)}) async-start(s8[10485760]{0:T(1024)(128)(4,1)} %bitcast.180), calls=%async_computation.16 | async-start | bytes 4194304
  21.4 6.6 %slice-start.7 = ((s8[10485760]{0:T(1024)(128)(4,1)}), s8[4194304]{0:T(1024)(128)(4,1)S(1)}, s32[]{:S(2)}) async-start(s8[10485760]{0:T(1024)(128)(4,1)} %bitcast.180), calls=%async_computation.17 | async-start | bytes 8388608
  21.5 6.9 %slice-start.8 = ((s8[10485760]{0:T(1024)(128)(4,1)}), s8[4194304]{0:T(1024)(128)(4,1)S(1)}, s32[]{:S(2)}) async-start(s8[10485760]{0:T(1024)(128)(4,1)} %bitcast.180), calls=%async_computation.18 | async-start | bytes 8388608
  31.6 6.6 %copy-start = (f32[2,32,1,128]{3,2,1,0:T(1,128)S(1)}, f32[2,32,1,128]{3,2,1,0:T(1,128)}, u32[]{:S(2)}) copy-start(f32[2,32,1,128]{3,2,1,0:T(1,128)} %param.5) | copy-start | bytes 98308
  32.9 36.9 %all-to-all-start.1 = ((bf16[4,2,32,1280]{3,2,1,0:T(8,128)(2,1)}), bf16[4,2,32,1280]{3,2,1,0:T(8,128)(2,1)S(1)}, u32[]{:S(2)}, u32[]{:S(2)}) async-start(bf16[4,2,32,1280]{3,2,1,0:T(8,128)(2,1)} %broadcast_in_dim.62), calls=%async_computation.1 | async-start | bytes 1310720 | tf_op jit(solution)/shard_map/all_to_all | solution.py:31
  69.8 17.9 %slice-start = ((s8[10485760]{0:T(1024)(128)(4,1)}), s8[2097152]{0:T(1024)(128)(4,1)S(1)}, s32[]{:S(2)}) async-start(s8[10485760]{0:T(1024)(128)(4,1)} %bitcast.176), calls=%async_computation.10 | async-start | bytes 4194304
  80.7 7.1 %slice-start.1 = ((s8[10485760]{0:T(1024)(128)(4,1)}), s8[4194304]{0:T(1024)(128)(4,1)S(1)}, s32[]{:S(2)}) async-start(s8[10485760]{0:T(1024)(128)(4,1)} %bitcast.176), calls=%async_computation.11 | async-start | bytes 8388608
  80.7 7.1 %slice-start.2 = ((s8[10485760]{0:T(1024)(128)(4,1)}), s8[4194304]{0:T(1024)(128)(4,1)S(1)}, s32[]{:S(2)}) async-start(s8[10485760]{0:T(1024)(128)(4,1)} %bitcast.176), calls=%async_computation.12 | async-start | bytes 8388608
  123.2 6.5 %slice-start.9 = ((s8[10485760]{0:T(1024)(128)(4,1)}), s8[2097152]{0:T(1024)(128)(4,1)S(1)}, s32[]{:S(2)}) async-start(s8[10485760]{0:T(1024)(128)(4,1)} %bitcast.182), calls=%async_computation.19 | async-start | bytes 4194304
  123.8 6.0 %slice-start.10 = ((s8[10485760]{0:T(1024)(128)(4,1)}), s8[4194304]{0:T(1024)(128)(4,1)S(1)}, s32[]{:S(2)}) async-start(s8[10485760]{0:T(1024)(128)(4,1)} %bitcast.182), calls=%async_computation.20 | async-start | bytes 8388608
  123.8 6.7 %slice-start.11 = ((s8[10485760]{0:T(1024)(128)(4,1)}), s8[4194304]{0:T(1024)(128)(4,1)S(1)}, s32[]{:S(2)}) async-start(s8[10485760]{0:T(1024)(128)(4,1)} %bitcast.182), calls=%async_computation.21 | async-start | bytes 8388608
  129.1 1.4 copy-start.2
  135.0 34.9 %all-to-all-start.5 = ((bf16[4,2,32,1280]{3,2,1,0:T(8,128)(2,1)}), bf16[4,2,32,1280]{3,2,1,0:T(8,128)(2,1)S(1)}, u32[]{:S(2)}, u32[]{:S(2)}) async-start(bf16[4,2,32,1280]{3,2,1,0:T(8,128)(2,1)} %broadcast_in_dim.66), calls=%async_computation.5 | async-start | bytes 1310720 | tf_op jit(solution)/shard_map/all_to_all | solution.py:31
  170.0 17.6 %slice-start.3 = ((s8[10485760]{0:T(1024)(128)(4,1)}), s8[2097152]{0:T(1024)(128)(4,1)S(1)}, s32[]{:S(2)}) async-start(s8[10485760]{0:T(1024)(128)(4,1)} %bitcast.178), calls=%async_computation.13 | async-start | bytes 4194304
  181.5 6.0 %slice-start.4 = ((s8[10485760]{0:T(1024)(128)(4,1)}), s8[4194304]{0:T(1024)(128)(4,1)S(1)}, s32[]{:S(2)}) async-start(s8[10485760]{0:T(1024)(128)(4,1)} %bitcast.178), calls=%async_computation.14 | async-start | bytes 8388608
  181.6 6.5 %slice-start.5 = ((s8[10485760]{0:T(1024)(128)(4,1)}), s8[4194304]{0:T(1024)(128)(4,1)S(1)}, s32[]{:S(2)}) async-start(s8[10485760]{0:T(1024)(128)(4,1)} %bitcast.178), calls=%async_computation.15 | async-start | bytes 8388608
  193.3 15.1 %all-to-all-start.7 = ((bf16[32,2,32,128]{3,2,1,0:T(8,128)(2,1)}), bf16[32,2,32,128]{3,2,1,0:T(8,128)(2,1)S(1)}, u32[]{:S(2)}, u32[]{:S(2)}) async-start(bf16[32,2,32,128]{3,2,1,0:T(8,128)(2,1)} %copy.262), calls=%async_computation.7 | async-start | bytes 1048576 | tf_op jit(solution)/shard_map/all_to_all | solution.py:19
  240.5 4.4 %copy-start.3 = (s32[160]{0:T(256)S(1)}, s32[160]{0:T(256)}, u32[]{:S(2)}) copy-start(s32[160]{0:T(256)} %param.9) | copy-start | bytes 1924
  240.5 38.8 %all-to-all-start.8 = ((f32[32,2,8,1280]{3,2,1,0:T(8,128)}), f32[32,2,8,1280]{3,2,1,0:T(8,128)S(1)}, u32[]{:S(2)}, u32[]{:S(2)}) async-start(f32[32,2,8,1280]{3,2,1,0:T(8,128)} %broadcast_in_dim.68), calls=%async_computation.8 | async-start | bytes 5242880 | tf_op jit(solution)/shard_map/all_to_all | solution.py:31
where the time goes:
time: 303 us; the launch traced here: 301 us
  blocking collectives  152 us (50%)
  waiting for transfers between devices  55.5 us (18%)
  matrix products  36.5 us (12%)
  starting transfers between devices  24.5 us (8%)
  local copies, waits for them, and re-layouts  23 us (8%)
  other arithmetic  8.98 us (3%)
    psum x12, blocking collectives, by_axis(): x = lax.psum(x, axis)  91.2 us
    all_to_all x4, blocking collectives, copy_for_each(): return lax.all_to_all(copies, axis, split_axis=0, concat_axis=0, tiled=True)  46 us
    all_to_all x4, waiting for transfers between devices, copy_for_each(): return lax.all_to_all(copies, axis, split_axis=0, concat_axis=0, tiled=True)  44.4 us
    all_to_all x4, starting transfers between devices, copy_for_each(): return lax.all_to_all(copies, axis, split_axis=0, concat_axis=0, tiled=True)  20.6 us
    all_to_all x1, blocking collectives, sent_and_summed(): tiles = lax.all_to_all(cut_along(x, dim, devices), axis, 0, 0, tiled=True)  14.5 us
    dot_general x2, matrix products, adjoint_terms(): jnp.einsum('ipcnk,dsin->ipcdsk', u_factor, data_b, preferred_element_type...  11.3 us
    all_to_all x1, waiting for transfers between devices, sent_and_summed(): tiles = lax.all_to_all(cut_along(x, dim, devices), axis, 0, 0, tiled=True)  11.1 us
    dot_general x2, matrix products, on_device(): jnp.einsum('ipcnk,dspn->ipcdsk', v_factor, model_b, preferred_element_typ...  10.6 us
  transfers between devices with their start and end apart: 5, of which 3 were waited for; matrix products, arithmetic and copies ran while one was open for 0% of the time, Pallas kernels for 0%

commit v1 on v0

--- a/solution.py
+++ b/solution.py
@@ -142,7 +142,10 @@
     own_share = lax.dynamic_slice_in_dim(x_vec, lax.axis_index("row") * share, share, 1)
     gathered = collect(own_share, COL, 2)
     gathered = gathered.reshape(2, share, all_cols, tile_size)
-    picked = jnp.take(gathered, where_held, axis=2).reshape(2, share, tile_cols * tile_size)
+    picked = jnp.concatenate(
+        [lax.dynamic_slice_in_dim(gathered, where_held[j], 1, axis=2) for j in range(tile_cols)],
+        axis=2,
+    ).reshape(2, share, tile_cols * tile_size)
     solution = collect(picked, "row", 1)
     return (solution, phibar)
 

time: 303 us -> 298 us (0.983)
  waiting for transfers between devices: 55.5 us -> 45.6 us
  between operations: 1.28 us -> 10.6 us
  local copies, waits for them, and re-layouts: 23 us -> 18.5 us
    all_to_all x4, waiting for transfers between devices: 44.4 us -> 34.5 us  [copy_for_each(): return lax.all_to_all(copies, axis, split_axis=0, concat_axis=0, tiled=True)]
  transfers between devices with their start and end apart: 5 -> 5, of which waited for: 3 -> 3; matrix products, arithmetic and copies ran while one was open for 0% -> 1% of each run, Pallas kernels for 0% -> 0%
where the time goes in v1:
time: 298 us; the launch traced here: 296 us
  blocking collectives  152 us (51%)
  waiting for transfers between devices  45.6 us (15%)
  matrix products  36.5 us (12%)
  starting transfers between devices  24.5 us (8%)
  local copies, waits for them, and re-layouts  18.5 us (6%)
  between operations  10.6 us (4%)
  other arithmetic  8.95 us (3%)
    psum x12, blocking collectives, by_axis(): x = lax.psum(x, axis)  91.2 us
    all_to_all x4, blocking collectives, copy_for_each(): return lax.all_to_all(copies, axis, split_axis=0, concat_axis=0, tiled=True)  46 us
    all_to_all x4, waiting for transfers between devices, copy_for_each(): return lax.all_to_all(copies, axis, split_axis=0, concat_axis=0, tiled=True)  34.5 us
    all_to_all x4, starting transfers between devices, copy_for_each(): return lax.all_to_all(copies, axis, split_axis=0, concat_axis=0, tiled=True)  20.6 us
    all_to_all x1, blocking collectives, sent_and_summed(): tiles = lax.all_to_all(cut_along(x, dim, devices), axis, 0, 0, tiled=True)  14.5 us
    dot_general x2, matrix products, adjoint_terms(): jnp.einsum('ipcnk,dsin->ipcdsk', u_factor, data_b, preferred_element_type...  11.3 us
    all_to_all x1, waiting for transfers between devices, sent_and_summed(): tiles = lax.all_to_all(cut_along(x, dim, devices), axis, 0, 0, tiled=True)  11.1 us
    dot_general x2, matrix products, on_device(): jnp.einsum('ipcnk,dspn->ipcdsk', v_factor, model_b, preferred_element_typ...  10.6 us
  transfers between devices with their start and end apart: 5, of which 3 were waited for; matrix products, arithmetic and copies ran while one was open for 1% of the time, Pallas kernels for 0%

profile of v1, /device:TPU:0, one launch (start us, length us, event | category | flops | bytes accessed | tf_op | source)
XLA Modules:
  0.0 296.3 jit_solution(509928026007286434)
XLA Ops:
  0.6 0.8 convert_element_type.53
  1.4 0.9 broadcast_in_dim.18
  2.3 7.4 %all-to-all-start = ((bf16[32,2,32,128]{3,2,1,0:T(8,128)(2,1)}), bf16[32,2,32,128]{3,2,1,0:T(8,128)(2,1)S(1)}, u32[]{:S(2)}, u32[]{:S(2)}) async-start(bf16[32,2,32,128]{3,2,1,0:T(8,128)(2,1)} %broadcast_in_dim.18), calls=%async_computation | async-start | bytes 1048576 | tf_op jit(solution)/shard_map/all_to_all | solution.py:31
  9.7 0.8 copy.220
  10.6 10.3 %all-to-all-done = bf16[32,2,32,128]{3,2,1,0:T(8,128)(2,1)S(1)} async-done(((bf16[32,2,32,128]{3,2,1,0:T(8,128)(2,1)}), bf16[32,2,32,128]{3,2,1,0:T(8,128)(2,1)S(1)}, u32[]{:S(2)}, u32[]{:S(2)}) %all-to-all-start) | async-done | bytes 524320 | tf_op jit(solution)/shard_map/all_to_all | solution.py:31
  20.9 0.3 copy.216
  21.3 0.2 reshape_reshape.9
  21.5 6.0 %fusion.29 = f32[16,5,2,2,32,128]{5,4,2,1,3,0:T(8,128)S(1)} fusion(bf16[16,5,2,256,128]{4,3,2,1,0:T(8,128)(2,1)} %param.6, bf16[2,32,16,256,1,1]{3,2,1,0,5,4:T(8,128)(2,1)S(1)} %bitcast.188), kind=kOutput, calls=%fused_computation.27 | convolution fusion | flops 671088640 | bytes 16252928 | tf_op jit(solution)/shard_map/ipcnk,dsin->ipcdsk/dot_general | solution.py:69
  27.4 0.3 fusion.48
  27.7 0.3 fusion.50
  28.0 0.3 slice-done.8
  28.3 3.3 %fusion.55 = f32[2,2,32,5,256]{4,2,0,1,3:T(8,128)S(1)} fusion(bf16[16,5,2,256,128]{4,3,2,1,0:T(8,128)(2,1)S(1)} %bitcast.180, f32[16,5,1,32,128]{4,3,1,0,2:T(8,128)S(1)} %fusion.48, f32[16,5,1,32,128]{4,3,1,0,2:T(8,128)S(1)} %fusion.50, f32[16,5,128]{2,1,0:T(8,128)S(1)} %fusion.88), kind=kOutput, calls=%fused_computation.58 | convolution fusion | flops 673054720 | bytes 13803520 | tf_op jit(solution)/shard_map/ipcnk,ipdsk->cdspn/dot_general | solution.py:74
  32.0 0.9 broadcast_in_dim.19
  32.9 5.3 %all-to-all-start.1 = ((bf16[4,2,32,1280]{3,2,1,0:T(8,128)(2,1)}), bf16[4,2,32,1280]{3,2,1,0:T(8,128)(2,1)S(1)}, u32[]{:S(2)}, u32[]{:S(2)}) async-start(bf16[4,2,32,1280]{3,2,1,0:T(8,128)(2,1)} %broadcast_in_dim.19), calls=%async_computation.1 | async-start | bytes 1310720 | tf_op jit(solution)/shard_map/all_to_all | solution.py:31
  38.3 8.9 %psum.84 = f32[32]{0:T(128)S(1)} all-reduce(f32[32]{0:T(128)S(1)} %multiply_reduce_fusion.4), channel_id=1, replica_groups=mesh['col_0'=4,'col_1'=4,'col_2'=2,'row'=4] {'col_0'}, use_global_device_ids=true, to_apply=%region_2.0 | all-reduce | flops 32 | bytes 256 | tf_op jit(solution)/shard_map/psum | solution.py:40
  47.2 9.2 %psum.85 = f32[32]{0:T(128)S(1)} all-reduce(f32[32]{0:T(128)S(1)} %psum.84), channel_id=1, replica_groups=mesh['col_0'=4,'col_1'=4,'col_2'=2,'row'=4] {'col_1'}, use_global_device_ids=true, to_apply=%region_3.0 | all-reduce | flops 32 | bytes 256 | tf_op jit(solution)/shard_map/psum | solution.py:40
  56.4 2.4 psum.86
  58.9 10.9 %psum.87 = f32[32]{0:T(128)S(1)} all-reduce(f32[32]{0:T(128)S(1)} %psum.86), channel_id=1, replica_groups=mesh['col_0'=4,'col_1'=4,'col_2'=2,'row'=4] {'row'}, use_global_device_ids=true, to_apply=%region_5.0 | all-reduce | flops 32 | bytes 256 | tf_op jit(solution)/shard_map/psum | solution.py:40
  69.9 0.2 multiply_reduce_fusion.1
  70.2 10.5 %all_to_all.52 = f32[32,1,32]{2,1,0:T(1,128)S(1)} all-to-all(f32[32,1,32]{2,1,0:T(1,128)S(1)} %broadcast_in_dim.21), channel_id=1, replica_groups=mesh['col_0'=4,'col_1'=4,'col_2'=2,'row'=4] {'col_0','col_1','col_2'}, dimensions={0} | all-to-all | bytes 8192 | tf_op jit(solution)/shard_map/all_to_all | solution.py:31
  80.7 5.3 %fusion.20 = f32[16,5,2,2,32,128]{5,4,1,0,3,2:T(8,128)S(1)} fusion(f32[2,4,5,8,256]{4,3,2,1,0:T(8,128)S(1)} %bitcast.184, f32[32]{0:T(128)S(1)} %sqrt.30, f32[32]{0:T(128)S(1)} %get-tuple-element.39, f32[32]{0:T(128)S(1)} %get-tuple-element.38, bf16[16,5,2,256,128]{4,3,2,1,0:T(8,128)(2,1)} %param.7), kind=kOutput, calls=%fused_computation.24 | convolution fusion | flops 671416320 | bytes 16056704 | tf_op jit(solution)/shard_map/ipcnk,dspn->ipcdsk/dot_general | solution.py:102
  86.0 1.7 fusion.47
  87.7 4.6 %fusion.32 = f32[2,2,32,16,256]{4,2,0,1,3:T(8,128)S(1)} fusion(bf16[16,5,2,256,128]{4,3,2,1,0:T(8,128)(2,1)S(1)} %bitcast.176, f32[16,5,1,32,128]{4,3,1,0,2:T(8,128)} %get-tuple-element.16, f32[16,5,1,32,128]{4,3,1,0,2:T(8,128)S(1)} %get-tuple-element.15, f32[16,5,128]{2,1,0:T(8,128)S(1)} %fusion.88), kind=kOutput, calls=%fused_computation.28 | convolution fusion | flops 673054720 | bytes 15245312 | tf_op jit(solution)/shard_map/ipcnk,ipdsk->cdsin/dot_general | solution.py:113
  93.1 0.2 copy.234
  93.3 14.5 %all_to_all.53 = bf16[32,2,32,128]{3,2,1,0:T(8,128)(2,1)S(1)} all-to-all(bf16[32,2,32,128]{3,2,1,0:T(8,128)(2,1)S(1)} %copy.234), channel_id=1, replica_groups=mesh['col_0'=4,'col_1'=4,'col_2'=2,'row'=4] {'col_0','col_1','col_2'}, dimensions={0} | all-to-all | bytes 1048576 | tf_op jit(solution)/shard_map/all_to_all | solution.py:19
  107.9 0.2 multiply_reduce_fusion.3
  108.2 15.0 %all_to_all.54 = bf16[32,2,32,128]{3,2,1,0:T(8,128)(2,1)S(1)} all-to-all(bf16[32,2,32,128]{3,2,1,0:T(8,128)(2,1)S(1)} %broadcast_in_dim.22), channel_id=1, replica_groups=mesh['col_0'=4,'col_1'=4,'col_2'=2,'row'=4] {'col_0','col_1','col_2'}, dimensions={0} | all-to-all | bytes 1048576 | tf_op jit(solution)/shard_map/all_to_all | solution.py:31
  123.2 0.3 copy.235
  123.6 0.2 reshape_reshape.10
  123.8 5.3 %fusion.26 = f32[16,5,2,2,32,128]{5,4,1,0,3,2:T(8,128)S(1)} fusion(bf16[2,32,16,256,1,1]{3,2,1,0,5,4:T(8,128)(2,1)S(1)} %bitcast.186, bf16[16,5,2,256,128]{4,3,2,1,0:T(8,128)(2,1)} %param.6), kind=kOutput, calls=%fused_computation.26 | convolution fusion | flops 671088640 | bytes 16252928 | tf_op jit(solution)/shard_map/ipcnk,dsin->ipcdsk/dot_general | solution.py:69
  129.1 0.6 fusion.45
  129.8 0.7 slice-done.11
  130.5 3.3 %fusion.60 = f32[2,2,32,5,256]{4,2,0,1,3:T(8,128)S(1)} fusion(bf16[16,5,2,256,128]{4,3,2,1,0:T(8,128)(2,1)S(1)} %bitcast.182, f32[16,5,1,32,128]{4,3,1,0,2:T(8,128)S(1)} %get-tuple-element.14, f32[16,5,1,32,128]{4,3,1,0,2:T(8,128)S(1)} %get-tuple-element.13, f32[16,5,128]{2,1,0:T(8,128)S(1)} %copy-done.2), kind=kOutput, calls=%fused_computation.59 | convolution fusion | flops 673054720 | bytes 13803520 | tf_op jit(solution)/shard_map/ipcnk,ipdsk->cdspn/dot_general | solution.py:74
  134.1 0.9 broadcast_in_dim.23
  135.0 3.5 %all-to-all-start.5 = ((bf16[4,2,32,1280]{3,2,1,0:T(8,128)(2,1)}), bf16[4,2,32,1280]{3,2,1,0:T(8,128)(2,1)S(1)}, u32[]{:S(2)}, u32[]{:S(2)}) async-start(bf16[4,2,32,1280]{3,2,1,0:T(8,128)(2,1)} %broadcast_in_dim.23), calls=%async_computation.5 | async-start | bytes 1310720 | tf_op jit(solution)/shard_map/all_to_all | solution.py:31
  138.5 8.9 %psum.88 = f32[32]{0:T(128)S(1)} all-reduce(f32[32]{0:T(128)S(1)} %get-tuple-element.9), channel_id=1, replica_groups=mesh['col_0'=4,'col_1'=4,'col_2'=2,'row'=4] {'col_0'}, use_global_device_ids=true, to_apply=%region_10.0 | all-reduce | flops 32 | bytes 256 | tf_op jit(solution)/shard_map/psum | solution.py:40
  147.4 9.2 %psum.89 = f32[32]{0:T(128)S(1)} all-reduce(f32[32]{0:T(128)S(1)} %psum.88), channel_id=1, replica_groups=mesh['col_0'=4,'col_1'=4,'col_2'=2,'row'=4] {'col_1'}, use_global_device_ids=true, to_apply=%region_11.0 | all-reduce | flops 32 | bytes 256 | tf_op jit(solution)/shard_map/psum | solution.py:40
  156.6 2.4 psum.90
  159.1 10.9 %psum.91 = f32[32]{0:T(128)S(1)} all-reduce(f32[32]{0:T(128)S(1)} %psum.90), channel_id=1, replica_groups=mesh['col_0'=4,'col_1'=4,'col_2'=2,'row'=4] {'row'}, use_global_device_ids=true, to_apply=%region_13.0 | all-reduce | flops 32 | bytes 256 | tf_op jit(solution)/shard_map/psum | solution.py:40
  170.1 1.1 multiply_reduce_fusion
  171.2 10.3 %all_to_all.55 = f32[32,1,32]{2,1,0:T(1,128)S(1)} all-to-all(f32[32,1,32]{2,1,0:T(1,128)S(1)} %broadcast_in_dim.24), channel_id=1, replica_groups=mesh['col_0'=4,'col_1'=4,'col_2'=2,'row'=4] {'col_0','col_1','col_2'}, dimensions={0} | all-to-all | bytes 8192 | tf_op jit(solution)/shard_map/all_to_all | solution.py:31
  181.6 5.3 %fusion.23 = f32[16,5,2,2,32,128]{5,4,1,0,3,2:T(8,128)S(1)} fusion(f32[2,4,5,8,256]{4,3,2,1,0:T(8,128)S(1)} %bitcast.187, f32[32]{0:T(128)S(1)} %sqrt.33, f32[32]{0:T(128)S(1)} %sqrt.31, f32[2,4,5,8,256]{4,3,2,1,0:T(8,128)S(1)} %bitcast.185, f32[32]{0:T(128)S(1)} %sqrt.30, f32[32]{0:T(128)S(1)} %get-tuple-element.39, f32[32]{0:T(128)S(1)} %get-tuple-element.38, ...), kind=kOutput, calls=%fused_computation.25 | convolution fusion | flops 671744000 | bytes 16384640 | tf_op jit(solution)/shard_map/ipcnk,dspn->ipcdsk/dot_general | solution.py:102
  186.9 0.6 fusion.43
  187.6 0.5 slice-done.5
  188.1 3.5 %fusion.35 = f32[2,2,32,16,256]{4,2,0,1,3:T(8,128)S(1)} fusion(bf16[16,5,2,256,128]{4,3,2,1,0:T(8,128)(2,1)S(1)} %bitcast.178, f32[16,5,1,32,128]{4,3,1,0,2:T(8,128)S(1)} %get-tuple-element.12, f32[16,5,1,32,128]{4,3,1,0,2:T(8,128)S(1)} %get-tuple-element.11, f32[16,5,128]{2,1,0:T(8,128)S(1)} %copy-done.2), kind=kOutput, calls=%fused_computation.29 | convolution fusion | flops 673054720 | bytes 15245312 | tf_op jit(solution)/shard_map/ipcnk,ipdsk->cdsin/dot_general | solution.py:113
  192.3 1.0 copy.251
  193.3 3.9 %all-to-all-start.7 = ((bf16[32,2,32,128]{3,2,1,0:T(8,128)(2,1)}), bf16[32,2,32,128]{3,2,1,0:T(8,128)(2,1)S(1)}, u32[]{:S(2)}, u32[]{:S(2)}) async-start(bf16[32,2,32,128]{3,2,1,0:T(8,128)(2,1)} %copy.251), calls=%async_computation.7 | async-start | bytes 1048576 | tf_op jit(solution)/shard_map/all_to_all | solution.py:19
  197.3 11.1 %all-to-all-done.7 = bf16[32,2,32,128]{3,2,1,0:T(8,128)(2,1)S(1)} async-done(((bf16[32,2,32,128]{3,2,1,0:T(8,128)(2,1)}), bf16[32,2,32,128]{3,2,1,0:T(8,128)(2,1)S(1)}, u32[]{:S(2)}, u32[]{:S(2)}) %all-to-all-start.7) | async-done | bytes 524320 | tf_op jit(solution)/shard_map/all_to_all | solution.py:19
  208.5 0.2 multiply_reduce_fusion.2
  208.6 8.9 %psum.92 = f32[32]{0:T(128)S(1)} all-reduce(f32[32]{0:T(128)S(1)} %multiply_reduce_fusion.2), channel_id=1, replica_groups=mesh['col_0'=4,'col_1'=4,'col_2'=2,'row'=4] {'col_0'}, use_global_device_ids=true, to_apply=%region_19.0 | all-reduce | flops 32 | bytes 256 | tf_op jit(solution)/shard_map/psum | solution.py:40
  217.6 9.2 %psum.93 = f32[32]{0:T(128)S(1)} all-reduce(f32[32]{0:T(128)S(1)} %psum.92), channel_id=1, replica_groups=mesh['col_0'=4,'col_1'=4,'col_2'=2,'row'=4] {'col_1'}, use_global_device_ids=true, to_apply=%region_20.0 | all-reduce | flops 32 | bytes 256 | tf_op jit(solution)/shard_map/psum | solution.py:40
  226.7 2.4 psum.94
  229.2 7.7 %psum.95 = f32[32]{0:T(128)S(1)} all-reduce(f32[32]{0:T(128)S(1)} %psum.94), channel_id=1, replica_groups=mesh['col_0'=4,'col_1'=4,'col_2'=2,'row'=4] {'row'}, use_global_device_ids=true, to_apply=%region_22.0 | all-reduce | flops 32 | bytes 256 | tf_op jit(solution)/shard_map/psum | solution.py:40
  236.9 0.6 divide_multiply_fusion
  237.7 1.0 fusion.87
  238.7 1.8 broadcast_in_dim.25
  240.5 4.4 %all-to-all-start.8 = ((f32[32,2,8,1280]{3,2,1,0:T(8,128)}), f32[32,2,8,1280]{3,2,1,0:T(8,128)S(1)}, u32[]{:S(2)}, u32[]{:S(2)}) async-start(f32[32,2,8,1280]{3,2,1,0:T(8,128)} %broadcast_in_dim.25), calls=%async_computation.8 | async-start | bytes 5242880 | tf_op jit(solution)/shard_map/all_to_all | solution.py:31
  245.0 0.2 select_reduce_fusion
  245.2 0.7 fusion.91
  255.2 24.1 %all-to-all-done.8 = f32[32,2,8,1280]{3,2,1,0:T(8,128)S(1)} async-done(((f32[32,2,8,1280]{3,2,1,0:T(8,128)}), f32[32,2,8,1280]{3,2,1,0:T(8,128)S(1)}, u32[]{:S(2)}, u32[]{:S(2)}) %all-to-all-start.8) | async-done | bytes 2621472 | tf_op jit(solution)/shard_map/all_to_all | solution.py:31
  279.4 3.0 %copy.252 = f32[2,8,32,1280]{3,2,1,0:T(8,128)} copy(f32[2,8,32,1280]{3,1,0,2:T(8,128)S(1)} %bitcast.183) | data formatting | bytes 5242880 | tf_op jit(solution)/shard_map/transpose | solution.py:24
  282.4 2.7 reshape_reshape.11
  285.4 10.1 %all_to_all.56 = f32[4,2,8,1280]{3,2,1,0:T(8,128)S(1)} all-to-all(f32[4,2,8,1280]{3,2,1,0:T(8,128)S(1)} %broadcast_in_dim.52), channel_id=1, replica_groups=mesh['col_0'=4,'col_1'=4,'col_2'=2,'row'=4] {'row'}, dimensions={0} | all-to-all | bytes 655360 | tf_op jit(solution)/shard_map/all_to_all | solution.py:31
  295.5 0.7 copy.367
  (85 shorter events, 3.6 us)
Async XLA Ops:
  2.3 18.6 %all-to-all-start = ((bf16[32,2,32,128]{3,2,1,0:T(8,128)(2,1)}), bf16[32,2,32,128]{3,2,1,0:T(8,128)(2,1)S(1)}, u32[]{:S(2)}, u32[]{:S(2)}) async-start(bf16[32,2,32,128]{3,2,1,0:T(8,128)(2,1)} %broadcast_in_dim.18), calls=%async_computation | async-start | bytes 1048576 | tf_op jit(solution)/shard_map/all_to_all | solution.py:31
  10.6 77.2 %copy-start.1 = (f32[16,5,128]{2,1,0:T(8,128)}, f32[16,5,128]{2,1,0:T(8,128)S(1)}, u32[]{:S(2)}) copy-start(f32[16,5,128]{2,1,0:T(8,128)S(1)} %fusion.88) | copy-start | bytes 122884
  21.2 6.8 %slice-start.6 = ((s8[10485760]{0:T(1024)(128)(4,1)}), s8[2097152]{0:T(1024)(128)(4,1)S(1)}, s32[]{:S(2)}) async-start(s8[10485760]{0:T(1024)(128)(4,1)} %bitcast.179), calls=%async_computation.16 | async-start | bytes 4194304
  21.4 6.6 %slice-start.7 = ((s8[10485760]{0:T(1024)(128)(4,1)}), s8[4194304]{0:T(1024)(128)(4,1)S(1)}, s32[]{:S(2)}) async-start(s8[10485760]{0:T(1024)(128)(4,1)} %bitcast.179), calls=%async_computation.17 | async-start | bytes 8388608
  21.5 6.9 %slice-start.8 = ((s8[10485760]{0:T(1024)(128)(4,1)}), s8[4194304]{0:T(1024)(128)(4,1)S(1)}, s32[]{:S(2)}) async-start(s8[10485760]{0:T(1024)(128)(4,1)} %bitcast.179), calls=%async_computation.18 | async-start | bytes 8388608
  31.6 6.6 %copy-start = (f32[2,32,1,128]{3,2,1,0:T(1,128)S(1)}, f32[2,32,1,128]{3,2,1,0:T(1,128)}, u32[]{:S(2)}) copy-start(f32[2,32,1,128]{3,2,1,0:T(1,128)} %param.5) | copy-start | bytes 98308
  32.9 36.9 %all-to-all-start.1 = ((bf16[4,2,32,1280]{3,2,1,0:T(8,128)(2,1)}), bf16[4,2,32,1280]{3,2,1,0:T(8,128)(2,1)S(1)}, u32[]{:S(2)}, u32[]{:S(2)}) async-start(bf16[4,2,32,1280]{3,2,1,0:T(8,128)(2,1)} %broadcast_in_dim.19), calls=%async_computation.1 | async-start | bytes 1310720 | tf_op jit(solution)/shard_map/all_to_all | solution.py:31
  69.8 17.9 %slice-start = ((s8[10485760]{0:T(1024)(128)(4,1)}), s8[2097152]{0:T(1024)(128)(4,1)S(1)}, s32[]{:S(2)}) async-start(s8[10485760]{0:T(1024)(128)(4,1)} %bitcast.175), calls=%async_computation.10 | async-start | bytes 4194304
  80.7 7.1 %slice-start.1 = ((s8[10485760]{0:T(1024)(128)(4,1)}), s8[4194304]{0:T(1024)(128)(4,1)S(1)}, s32[]{:S(2)}) async-start(s8[10485760]{0:T(1024)(128)(4,1)} %bitcast.175), calls=%async_computation.11 | async-start | bytes 8388608
  80.7 7.1 %slice-start.2 = ((s8[10485760]{0:T(1024)(128)(4,1)}), s8[4194304]{0:T(1024)(128)(4,1)S(1)}, s32[]{:S(2)}) async-start(s8[10485760]{0:T(1024)(128)(4,1)} %bitcast.175), calls=%async_computation.12 | async-start | bytes 8388608
  123.2 6.5 %slice-start.9 = ((s8[10485760]{0:T(1024)(128)(4,1)}), s8[2097152]{0:T(1024)(128)(4,1)S(1)}, s32[]{:S(2)}) async-start(s8[10485760]{0:T(1024)(128)(4,1)} %bitcast.181), calls=%async_computation.19 | async-start | bytes 4194304
  123.8 6.0 %slice-start.10 = ((s8[10485760]{0:T(1024)(128)(4,1)}), s8[4194304]{0:T(1024)(128)(4,1)S(1)}, s32[]{:S(2)}) async-start(s8[10485760]{0:T(1024)(128)(4,1)} %bitcast.181), calls=%async_computation.20 | async-start | bytes 8388608
  123.8 6.7 %slice-start.11 = ((s8[10485760]{0:T(1024)(128)(4,1)}), s8[4194304]{0:T(1024)(128)(4,1)S(1)}, s32[]{:S(2)}) async-start(s8[10485760]{0:T(1024)(128)(4,1)} %bitcast.181), calls=%async_computation.21 | async-start | bytes 8388608
  129.1 1.4 copy-start.2
  135.0 34.9 %all-to-all-start.5 = ((bf16[4,2,32,1280]{3,2,1,0:T(8,128)(2,1)}), bf16[4,2,32,1280]{3,2,1,0:T(8,128)(2,1)S(1)}, u32[]{:S(2)}, u32[]{:S(2)}) async-start(bf16[4,2,32,1280]{3,2,1,0:T(8,128)(2,1)} %broadcast_in_dim.23), calls=%async_computation.5 | async-start | bytes 1310720 | tf_op jit(solution)/shard_map/all_to_all | solution.py:31
  170.0 17.6 %slice-start.3 = ((s8[10485760]{0:T(1024)(128)(4,1)}), s8[2097152]{0:T(1024)(128)(4,1)S(1)}, s32[]{:S(2)}) async-start(s8[10485760]{0:T(1024)(128)(4,1)} %bitcast.177), calls=%async_computation.13 | async-start | bytes 4194304
  181.5 6.0 %slice-start.4 = ((s8[10485760]{0:T(1024)(128)(4,1)}), s8[4194304]{0:T(1024)(128)(4,1)S(1)}, s32[]{:S(2)}) async-start(s8[10485760]{0:T(1024)(128)(4,1)} %bitcast.177), calls=%async_computation.14 | async-start | bytes 8388608
  181.6 6.5 %slice-start.5 = ((s8[10485760]{0:T(1024)(128)(4,1)}), s8[4194304]{0:T(1024)(128)(4,1)S(1)}, s32[]{:S(2)}) async-start(s8[10485760]{0:T(1024)(128)(4,1)} %bitcast.177), calls=%async_computation.15 | async-start | bytes 8388608
  193.3 15.1 %all-to-all-start.7 = ((bf16[32,2,32,128]{3,2,1,0:T(8,128)(2,1)}), bf16[32,2,32,128]{3,2,1,0:T(8,128)(2,1)S(1)}, u32[]{:S(2)}, u32[]{:S(2)}) async-start(bf16[32,2,32,128]{3,2,1,0:T(8,128)(2,1)} %copy.251), calls=%async_computation.7 | async-start | bytes 1048576 | tf_op jit(solution)/shard_map/all_to_all | solution.py:19
  240.5 4.4 %copy-start.3 = (s32[160]{0:T(256)S(1)}, s32[160]{0:T(256)}, u32[]{:S(2)}) copy-start(s32[160]{0:T(256)} %param.9) | copy-start | bytes 1924
  240.5 38.8 %all-to-all-start.8 = ((f32[32,2,8,1280]{3,2,1,0:T(8,128)}), f32[32,2,8,1280]{3,2,1,0:T(8,128)S(1)}, u32[]{:S(2)}, u32[]{:S(2)}) async-start(f32[32,2,8,1280]{3,2,1,0:T(8,128)} %broadcast_in_dim.25), calls=%async_computation.8 | async-start | bytes 5242880 | tf_op jit(solution)/shard_map/all_to_all | solution.py:31

commit v2 on v0

v2 whole, which is shorter than its diff:
```python
import functools
import math

import jax
import jax.numpy as jnp
from jax import lax
from jax.experimental import pallas as pl
from jax.experimental.pallas import tpu as pltpu
from jax.sharding import PartitionSpec as P

F32 = jnp.float32
BF16 = jnp.bfloat16
MESH = pl.DeviceIdType.MESH
LANES = 128
GROUP = 2


def nn(lhs, rhs):
    return jnp.dot(lhs, rhs, preferred_element_type=F32)


def nt(lhs, rhs):
    return lax.dot_general(lhs, rhs, (((1,), (1,)), ((), ())), preferred_element_type=F32)


def lanes(*parts):
    return jnp.concatenate(parts, axis=1)


def stacked(*parts):
    return jnp.concatenate(parts, axis=0)


def times_factor(vec):
    half = vec.shape[0] // 2
    re, im = vec[:half], vec[half:]
    return stacked(lanes(re, -im), lanes(im, re))


def times_conj_factor(vec):
    half = vec.shape[0] // 2
    re, im = vec[:half], vec[half:]
    return stacked(lanes(re, im), lanes(im, -re))


def to_row(acc):
    pad = jnp.zeros((LANES - acc.shape[0], LANES), F32)
    return jnp.sum(stacked(acc, pad).T, axis=0, keepdims=True)


def to_col(row, sources):
    col = jnp.broadcast_to(row, (LANES, LANES)).T[:sources]
    return stacked(col, col)


def kernel(
    dims,
    rhs,
    u_hbm,
    v_hbm,
    ranks,
    assign,
    out,
    phi_out,
    d_out,
    v_own,
    u_fac,
    v_fac,
    d_full,
    y_send,
    y_recv,
    z_acc,
    z_send,
    z_recv,
    v_full,
    lhs_p,
    gathered0,
    gathered1,
    picked,
    sib_recv,
    natural,
    cols,
    row_send,
    row_recv,
    zrow_send,
    zrow_recv,
    fac_sem,
    ag_s,
    ag_r,
    ys_s,
    ys_r,
    row_s,
    row_r,
    zr_s,
    zr_r,
    zs_s,
    zs_r,
    zg_s,
    zg_r,
    ng_s,
    ng_r,
    sib_s,
    sib_r,
    nz_s,
    nz_r,
):
    chips, nx, ny, nz, tile_cols, sources = dims
    rows = 2 * sources
    zrows = rows // nz
    gathered = (gathered0, gathered1)
    me_c, me_z = lax.axis_index("col"), lax.axis_index("row")
    chip, core = lax.div(me_c, 2), lax.rem(me_c, 2)
    cx, cy = lax.div(chip, ny), lax.rem(chip, ny)

    def chip_to(q):
        return lax.rem(cx + lax.div(q, ny), nx) * ny + lax.rem(cy + lax.rem(q, ny), ny)

    def chip_from(q):
        return lax.rem(cx + nx - lax.div(q, ny), nx) * ny + lax.rem(cy + ny - lax.rem(q, ny), ny)

    def remote(src, dst, send, recv, col, row):
        return pltpu.make_async_remote_copy(
            src_ref=src, dst_ref=dst, send_sem=send, recv_sem=recv,
            device_id=(col, row), device_id_type=MESH,
        )

    def in_plane(k):
        return chip_to(lax.div(k, 2)) * 2 + lax.rem(core + lax.rem(k, 2), 2)

    def along_z(k):
        return lax.rem(me_z + k, nz)

    def copy_ag(rd, k):
        own = d_full.at[rd, chip, core]
        return remote(own, own, ag_s.at[rd, k], ag_r.at[rd, k], in_plane(k), me_z)

    def copy_ys(rd, k):
        to_chip, to_core = chip_to(lax.div(k, 2)), lax.rem(core + lax.rem(k, 2), 2)
        return remote(
            y_send.at[rd, to_chip, to_core], y_recv.at[rd, k], ys_s.at[rd, k], ys_r.at[rd, k],
            to_chip * 2 + to_core, me_z,
        )

    def copy_row(rd, k):
        return remote(
            row_send.at[rd], row_recv.at[rd, k], row_s.at[rd, k], row_r.at[rd, k], in_plane(k), me_z
        )

    def copy_zrow(rd, k):
        return remote(
            zrow_send.at[rd], zrow_recv.at[rd, k], zr_s.at[rd, k], zr_r.at[rd, k], me_c, along_z(k)
        )

    def copy_zs(rd, k):
        return remote(
            z_send.at[rd, along_z(k)], z_recv.at[rd, k], zs_s.at[rd, k], zs_r.at[rd, k], me_c,
            along_z(k),
        )

    def copy_zg(rd, k):
        own = v_full.at[rd, me_z]
        return remote(own, own, zg_s.at[rd, k], zg_r.at[rd, k], me_c, along_z(k))

    def copy_ng(rd, q):
        own = gathered[rd].at[pl.ds(chip * tile_cols, tile_cols)]
        return remote(own, own, ng_s.at[rd, q], ng_r.at[rd, q], chip_to(q) * 2 + core, me_z)

    def copy_sib(rd):
        return remote(
            picked.at[rd, 1 - core], sib_recv.at[rd], sib_s.at[rd], sib_r.at[rd],
            chip * 2 + 1 - core, me_z,
        )

    def copy_nz(rd, k):
        own = natural.at[rd, me_z]
        return remote(own, own, nz_s.at[rd, k], nz_r.at[rd, k], me_c, along_z(k))

    def loop(low, high, body):
        lax.fori_loop(low, high, lambda i, c: (body(i), c)[1], 0)

    def factor_copies(i):
        return (
            pltpu.make_async_copy(u_hbm.at[i], u_fac.at[i], fac_sem.at[0, i]),
            pltpu.make_async_copy(v_hbm.at[i], v_fac.at[i], fac_sem.at[1, i]),
        )

    lane = lax.broadcasted_iota(jnp.int32, (rows, LANES), 1)

    def masked(value, i, p):
        return jnp.where(lane < ranks[i, p], value, 0.0).astype(BF16)

    def lane_sums(square, acc):
        for at in range(0, square.shape[1], LANES):
            part = square[:, at : at + LANES]
            acc = acc + part[:sources] + part[sources:]
        return acc

    def start_factor(q):
        for copy in factor_copies(chip_from(q)):
            copy.start()

    loop(0, chips, start_factor)
    d_full[0, chip, core] = rhs[...].astype(BF16)

    barrier = pltpu.get_barrier_semaphore()

    def greet(k):
        pl.semaphore_signal(barrier, inc=1, device_id=(in_plane(k), me_z), device_id_type=MESH)

    def greet_z(k):
        pl.semaphore_signal(barrier, inc=1, device_id=(me_c, along_z(k)), device_id_type=MESH)

    loop(1, 2 * chips, greet)
    loop(1, nz, greet_z)
    pl.semaphore_wait(barrier, 2 * chips - 1 + nz - 1)
    loop(1, 2 * chips, lambda k: copy_ag(0, k).start())

    def adjoint(rd):
        z_acc[...] = jnp.zeros_like(z_acc)

        def group(g, acc):
            parts = [[] for _ in range(tile_cols)]
            where = []
            for j in range(GROUP):
                q = g * GROUP + j
                i = chip_from(q)
                where.append(i)

                @pl.when(q > 0)
                def _():
                    copy_ag(rd, 2 * q).wait_recv()

                copy_ag(rd, 2 * q + 1).wait_recv()
                if rd == 0:
                    for copy in factor_copies(i):
                        copy.wait()
                data = lanes(d_full[rd, i, 0], d_full[rd, i, 1])
                wide = data.astype(F32)
                acc = lane_sums(wide * wide, acc)
                left = times_conj_factor(data)
                right = lanes(*[u_fac[i, p].reshape(-1, LANES) for p in range(tile_cols)])
                raw = nn(left, right)
                for p in range(tile_cols):
                    coeff = masked(raw[:, p * LANES : (p + 1) * LANES], i, p)
                    parts[p].append(times_conj_factor(coeff))
            for p in range(tile_cols):
                right = lanes(*[v_fac[i, p, c] for i in where for c in range(2)])
                z_acc[p] += nt(lanes(*parts[p]), right)
            return acc

        return lax.fori_loop(0, chips // GROUP, group, jnp.zeros((sources, LANES), F32))

    def start_model(rd):
        for r in range(nz):
            z_send[rd, r] = z_acc[:, r * zrows : (r + 1) * zrows, :].astype(BF16)
        loop(1, nz, lambda k: copy_zs(rd, k).start())

    def zrow_start(rd, row):
        zrow_send[rd] = row
        loop(1, nz, lambda k: copy_zrow(rd, k).start())

    def zrow_sum(rd):
        total = zrow_send[rd]
        for k in range(1, nz):
            copy_zrow(rd, k).wait_recv()
            total = total + zrow_recv[rd, k]
        return total

    own_rows = pl.ds(pl.multiple_of(me_z * zrows, zrows), zrows)

    def own_col(slot):
        part = cols[slot, own_rows, :]
        return lanes(part, part)[None]

    def model_sum(rd):
        total = z_acc[:, own_rows, :]
        for k in range(1, nz):
            copy_zs(rd, k).wait_recv()
            total = total + z_recv[rd, k].astype(F32)
        return total

    def send_model(rd, v_hat):
        v_own[rd] = v_hat
        v_b = v_hat.astype(BF16)
        v_full[rd, me_z] = v_b
        loop(1, nz, lambda k: copy_zg(rd, k).start())
        gathered[rd][pl.ds(chip * tile_cols, tile_cols)] = v_b
        loop(1, chips, lambda q: copy_ng(rd, q).start())

    def forward(rd):
        for k in range(1, nz):
            copy_zg(rd, k).wait_recv()
        acc = jnp.zeros((sources, LANES), F32)
        for p in range(tile_cols):
            vec = stacked(*[v_full[rd, r, p] for r in range(nz)])
            wide = vec.astype(F32)
            acc = lane_sums(wide * wide, acc)
            lhs_p[p] = times_factor(vec)
        row_send[rd] = to_row(acc)
        loop(1, 2 * chips, lambda k: copy_row(rd, k).start())

        def group(g):
            qs = [chips - 1 - (g * GROUP + j) for j in range(GROUP)]
            where = [chip_to(q) for q in qs]
            parts = [[] for _ in range(GROUP)]
            for p in range(tile_cols):
                right = lanes(*[v_fac[i, p].reshape(-1, LANES) for i in where])
                raw = nn(lhs_p[p], right)
                for j, i in enumerate(where):
                    coeff = masked(raw[:, j * LANES : (j + 1) * LANES], i, p)
                    parts[j].append(times_factor(coeff))
            for j, i in enumerate(where):
                right = lanes(*[u_fac[i, p, c] for p in range(tile_cols) for c in range(2)])
                y = nt(lanes(*parts[j]), right).astype(BF16)
                y_send[rd, i, 0] = y[:, :LANES]
                y_send[rd, i, 1] = y[:, LANES:]

                @pl.when(qs[j] > 0)
                def _():
                    copy_ys(rd, 2 * qs[j]).start()

                copy_ys(rd, 2 * qs[j] + 1).start()

        loop(0, chips // GROUP, group)

    def row_sum(rd):
        def add(k, total):
            copy_row(rd, k).wait_recv()
            return total + row_recv[rd, k]

        return lax.fori_loop(1, 2 * chips, add, row_send[rd])

    def data_sum(rd):
        def add(k, total):
            copy_ys(rd, k).wait_recv()
            return total + y_recv[rd, k].astype(F32)

        return lax.fori_loop(1, 2 * chips, add, y_send[rd, chip, core].astype(F32))

    def pick(rd, held):
        for q in range(1, chips):
            copy_ng(rd, q).wait_recv()
        for j, (found, at) in enumerate(held):
            seg = gathered[rd][at].astype(F32) * found.astype(F32)
            picked[rd, j // tile_cols, j % tile_cols] = seg.astype(BF16)
        copy_sib(rd).start()

    def join(rd):
        copy_sib(rd).wait_recv()
        mine = picked[rd, core].astype(F32) + sib_recv[rd].astype(F32)
        natural[rd, me_z] = mine.astype(BF16)
        loop(1, nz, lambda k: copy_nz(rd, k).start())

    def find_held():
        first = chip * (2 * tile_cols)
        zero = jnp.int32(0)

        def step(a, carry):
            found, at = list(carry[0]), list(carry[1])
            for t in range(tile_cols):
                held = assign[a * (2 * tile_cols) + core * tile_cols + t] - first
                for j in range(2 * tile_cols):
                    hit = held == j
                    found[j] = jnp.where(hit, 1, found[j])
                    at[j] = jnp.where(hit, a * tile_cols + t, at[j])
            return tuple(found), tuple(at)

        many = 2 * tile_cols
        found, at = lax.fori_loop(0, chips, step, ((zero,) * many, (zero,) * many))
        return list(zip(found, at))

    acc = adjoint(0)
    start_model(0)
    zrow_start(0, to_row(acc))
    beta0 = jnp.sqrt(zrow_sum(0))
    cols[0] = to_col(beta0, sources)
    v_hat = model_sum(0) / own_col(0)
    send_model(0, v_hat)

    forward(0)
    held = find_held()
    alpha0 = jnp.sqrt(row_sum(0))
    cols[1] = to_col(alpha0, sources)
    d_hat = data_sum(0) / cols[1] - cols[1] * (rhs[...] / cols[0])
    d_full[1, chip, core] = d_hat.astype(BF16)
    loop(1, 2 * chips, lambda k: copy_ag(1, k).start())
    d_out[...] = d_hat
    pick(0, held)
    acc = adjoint(1)
    start_model(1)
    zrow_start(1, to_row(acc))
    join(0)
    beta1 = jnp.sqrt(zrow_sum(1))
    cols[2] = to_col(beta1, sources)
    v_hat = model_sum(1) / own_col(2) - own_col(2) * (v_own[0] / own_col(1))
    send_model(1, v_hat)

    forward(1)
    alpha1 = jnp.sqrt(row_sum(1))
    cols[3] = to_col(alpha1, sources)
    d_hat = data_sum(1) / cols[3] - cols[3] * (d_out[...] / cols[2])
    square = d_hat * d_hat
    row_send[2] = to_row(square[:sources] + square[sources:])
    loop(1, 2 * chips, lambda k: copy_row(2, k).start())
    d_out[...] = d_hat
    pick(1, held)
    zrow_start(2, row_sum(2))
    join(1)
    rho1 = jnp.sqrt(alpha0 * alpha0 + beta1 * beta1)
    cosine = alpha0 / rho1
    sine = beta1 / rho1
    theta = sine * alpha1
    rhobar = -cosine * alpha1
    phi1 = cosine * beta0
    phibar = sine * beta0
    beta2 = jnp.sqrt(zrow_sum(2))
    rho2 = jnp.sqrt(rhobar * rhobar + beta2 * beta2)
    cosine = rhobar / rho2
    sine = beta2 / rho2
    step2 = cosine * phibar / rho2
    phi_out[0:1] = sine * phibar
    phi_out[1:2] = sine / rho2
    phi_out[2:3] = theta / rho1
    phi_out[3:4] = alpha0
    phi_out[4:5] = alpha1
    first = to_col((phi1 / rho1 - step2 * (theta / rho1)) / alpha0, sources)
    second = to_col(step2 / alpha1, sources)
    for rd in range(2):
        for k in range(1, nz):
            copy_nz(rd, k).wait_recv()
    width = natural.shape[-1]
    for p in range(tile_cols):
        for at in range(0, width, LANES):
            one = stacked(*[natural[0, r, p, :, at : at + LANES] for r in range(nz)])
            two = stacked(*[natural[1, r, p, :, at : at + LANES] for r in range(nz)])
            out[:, p * width + at : p * width + at + LANES] = (
                first * one.astype(F32) + second * two.astype(F32)
            )

    for rd in range(2):
        loop(1, 2 * chips, lambda k, rd=rd: copy_ag(rd, k).wait_send())
        loop(1, 2 * chips, lambda k, rd=rd: copy_ys(rd, k).wait_send())
        loop(1, nz, lambda k, rd=rd: copy_zs(rd, k).wait_send())
        loop(1, nz, lambda k, rd=rd: copy_zg(rd, k).wait_send())
        loop(1, nz, lambda k, rd=rd: copy_nz(rd, k).wait_send())
        loop(1, chips, lambda k, rd=rd: copy_ng(rd, k).wait_send())
        copy_sib(rd).wait_send()
    for rd in range(3):
        loop(1, 2 * chips, lambda k, rd=rd: copy_row(rd, k).wait_send())
        loop(1, nz, lambda k, rd=rd: copy_zrow(rd, k).wait_send())


def last_adjoint(d_hat, v_hats, scalars, u_factor, v_factor, ranks):
    tile_rows, tile_cols, _, tile_size, rank_cap = u_factor.shape
    sources = d_hat.shape[0] // 2
    rank_iota = lax.broadcasted_iota(jnp.int32, (tile_rows, tile_cols, 1, 1, rank_cap), 4)
    mask = (rank_iota < ranks[:, :, None, None, None]).astype(F32)
    d_hat = d_hat.reshape(2, sources, -1)
    beta = jnp.sqrt(lax.psum(jnp.sum(d_hat * d_hat, axis=(0, 2)), ("col", "row")))
    data = lax.all_gather(d_hat.astype(BF16), "col", axis=2, tiled=True)
    data = data.reshape(2, sources, tile_rows, tile_size)
    raw = jnp.einsum("ipcnk,dsin->ipcdsk", u_factor, data, preferred_element_type=F32)
    coeff = jnp.stack([raw[:, :, 0, 0] + raw[:, :, 1, 1], raw[:, :, 0, 1] - raw[:, :, 1, 0]], axis=2)
    coeff = (coeff * mask).astype(BF16)
    prod = jnp.einsum("ipcnk,ipdsk->cdspn", v_factor, coeff, preferred_element_type=F32)
    model = jnp.stack([prod[0, 0] + prod[1, 1], prod[0, 1] - prod[1, 0]], axis=0)
    model = lax.psum(model, "row").reshape(2, sources, tile_cols * tile_size)
    sine_by_rho, theta_by_rho, alpha0, alpha1 = [row[None, :, None] for row in scalars]
    v_hats = lax.all_gather(v_hats, "row", axis=2, tiled=True)
    v_hats = v_hats.transpose(0, 2, 1, 3).reshape(2, *model.shape)
    v_prev = v_hats[1] / alpha1
    w_prev = v_prev - theta_by_rho * (v_hats[0] / alpha0)
    v_hat = model / beta[None, :, None] - beta[None, :, None] * v_prev
    alpha = jnp.sqrt(lax.psum(jnp.sum(v_hat * v_hat, axis=(0, 2)), "col"))
    v_vec = v_hat / alpha[None, :, None]
    return v_vec, alpha, v_vec - sine_by_rho * alpha[None, :, None] * w_prev


def on_device(nz, rhs, u_factor, v_factor, ranks, assign):
    tile_rows, tile_cols, _, tile_size, _ = u_factor.shape
    sources = rhs.shape[1]
    rows = 2 * sources
    zrows = rows // nz
    chips = tile_rows
    ny = math.isqrt(chips)
    nx = chips // ny
    dims = (chips, nx, ny, nz, tile_cols, sources)
    seg = (tile_cols, zrows, tile_size)
    dma = pltpu.SemaphoreType.DMA
    vmem = pl.BlockSpec(memory_space=pltpu.VMEM)
    smem = pl.BlockSpec(memory_space=pltpu.SMEM)
    hbm = pl.BlockSpec(memory_space=pl.ANY)
    peers, zs = (2, 2 * chips), (2, nz)
    out, scalars, d_hat, v_hats = pl.pallas_call(
        functools.partial(kernel, dims),
        out_shape=[
            jax.ShapeDtypeStruct((rows, tile_cols * tile_size), F32),
            jax.ShapeDtypeStruct((5, LANES), F32),
            jax.ShapeDtypeStruct((rows, LANES), F32),
            jax.ShapeDtypeStruct((2, *seg), F32),
        ],
        in_specs=[vmem, hbm, hbm, smem, smem],
        out_specs=[vmem] * 4,
        scratch_shapes=[
            pltpu.VMEM(u_factor.shape, BF16),
            pltpu.VMEM(v_factor.shape, BF16),
            pltpu.VMEM((2, chips, 2, rows, LANES), BF16),
            pltpu.VMEM((2, chips, 2, rows, LANES), BF16),
            pltpu.VMEM((2, 2 * chips, rows, LANES), BF16),
            pltpu.VMEM((tile_cols, rows, tile_size), F32),
            pltpu.VMEM((2, nz, *seg), BF16),
            pltpu.VMEM((2, nz, *seg), BF16),
            pltpu.VMEM((2, nz, *seg), BF16),
            pltpu.VMEM((tile_cols, rows, 2 * tile_size), BF16),
            pltpu.VMEM((chips * tile_cols, zrows, tile_size), BF16),
            pltpu.VMEM((chips * tile_cols, zrows, tile_size), BF16),
            pltpu.VMEM((2, 2, *seg), BF16),
            pltpu.VMEM((2, *seg), BF16),
            pltpu.VMEM((2, nz, *seg), BF16),
            pltpu.VMEM((4, rows, LANES), F32),
            pltpu.VMEM((3, 1, LANES), F32),
            pltpu.VMEM((3, 2 * chips, 1, LANES), F32),
            pltpu.VMEM((3, 1, LANES), F32),
            pltpu.VMEM((3, nz, 1, LANES), F32),
            dma((2, chips)),
            dma(peers), dma(peers),
            dma(peers), dma(peers),
            dma((3, 2 * chips)), dma((3, 2 * chips)),
            dma((3, nz)), dma((3, nz)),
            dma(zs), dma(zs),
            dma(zs), dma(zs),
            dma((2, chips)), dma((2, chips)),
            dma((2,)), dma((2,)),
            dma(zs), dma(zs),
        ],
        compiler_params=pltpu.CompilerParams(
            collective_id=0, has_side_effects=True, vmem_limit_bytes=58 * 2**20
        ),
        name="lsqr",
    )(rhs.reshape(rows, LANES), u_factor, v_factor, ranks, assign)
    last_adjoint(d_hat, v_hats, scalars[1:, :sources], u_factor, v_factor, ranks)
    phibar = scalars[0, :sources]
    return out.reshape(2, sources, tile_cols * tile_size), phibar


def solution(mesh):
    return jax.shard_map(
        functools.partial(on_device, mesh.shape["row"]),
        mesh=mesh,
        in_specs=(
            P(None, None, "row", "col"),
            P("row", "col", None, None, None),
            P("row", "col", None, None, None),
            P("row", "col"),
            P(),
        ),
        out_specs=(P(None, None, "col"), P()),
        check_vma=False,
    )
```

time: 303 us -> 104 us (0.34)
  blocking collectives: 152 us -> 0 us
  Pallas kernels: 0 us -> 98.8 us
  waiting for transfers between devices: 55.5 us -> 0 us
  matrix products: 36.5 us -> 0 us
  starting transfers between devices: 24.5 us -> 0 us
  local copies, waits for them, and re-layouts: 23 us -> 4.26 us
  other arithmetic: 8.98 us -> 0 us
    pallas_call x0 -> x1, Pallas kernels: none -> 98.8 us  [on_device(): pl.pallas_call(functools.partial(kernel, dims), out_shape=[jax.ShapeDtype...]
    psum x12 -> x0, blocking collectives: 91.2 us -> none  [by_axis(): x = lax.psum(x, axis)]
    all_to_all x5 -> x0, blocking collectives: 60.4 us -> none  [the longest x4 46 us: copy_for_each(): return lax.all_to_all(copies, axis, split_axis=0, concat_axis=0, tiled=True)]
    all_to_all x5 -> x0, waiting for transfers between devices: 55.5 us -> none  [the longest x4 44.4 us: copy_for_each(): return lax.all_to_all(copies, axis, split_axis=0, concat_axis=0, tiled=True)]
    dot_general x8 -> x0, matrix products: 36.5 us -> none  [the longest x2 11.3 us: adjoint_terms(): jnp.einsum('ipcnk,dsin->ipcdsk', u_factor, data_b, preferred_element_type...]
    all_to_all x5 -> x0, starting transfers between devices: 24.5 us -> none  [the longest x4 20.6 us: copy_for_each(): return lax.all_to_all(copies, axis, split_axis=0, concat_axis=0, tiled=True)]
    another operation x12 -> x0, local copies, waits for them, and re-layouts: 6.89 us -> none  [the longest x2 5.74 us: on_device(): gathered = gathered.reshape(2, share, all_cols, tile_size)]
    transpose x5 -> x0, local copies, waits for them, and re-layouts: 4.91 us -> none  [the longest x3 3.71 us: in_order(): tiles = jnp.moveaxis(tiles, 0, dim)]
  transfers between devices with their start and end apart: 5 -> 0, of which waited for: 3 -> 0; matrix products, arithmetic and copies ran while one was open for 0% -> 0% of each run, Pallas kernels for 0% -> 0%
where the time goes in v2:
time: 104 us
  Pallas kernels  98.8 us (95%)
  local copies, waits for them, and re-layouts  4.26 us (4%)
    pallas_call x1, Pallas kernels, on_device(): pl.pallas_call(functools.partial(kernel, dims), out_shape=[jax.ShapeDtype...  98.8 us
    unnamed x2, local copies, waits for them, and re-layouts  3.08 us

profile of v2, /device:TPU:0, one launch (start us, length us, event | category | flops | bytes accessed | tf_op | source)
XLA Modules:
  0.0 103.7 jit_solution(5789908301025801618)
XLA Ops:
  0.6 1.4 %copy.7.ranks = s32[16,5]{1,0:T(8,128)} copy(s32[16,5]{0,1:T(8,128)} %param.8) | data formatting | bytes 640 | tf_op args[3]
  2.0 98.8 %lsqr.1 = (f32[64,1280]{1,0:T(8,128)}, f32[5,128]{1,0:T(8,128)}, f32[64,128]{1,0:T(8,128)}, f32[2,5,16,256]{3,2,1,0:T(8,128)}) custom-call(f32[64,128]{1,0:T(8,128)} %bitcast.5, bf16[16,5,2,256,128]{4,3,2,1,0:T(8,128)(2,1)} %u_hbm.1, bf16[16,5,2,256,128]{4,3,2,1,0:T(8,128)(2,1)} %v_hbm.1, s32[16,5]{1,0:T(8,128)} %copy.7.ranks, s32[160]{0:T(256)} %assign.1), custom_call_target="tpu_custom_call" | custom-call | tf_op jit(solution)/shard_map/lsqr/pallas_call | solution.py:494
  100.8 1.2 %slice_bitcast_fusion = f32[32]{0:T(128)} fusion(f32[5,128]{1,0:T(8,128)} %get-tuple-element.5), kind=kLoop, calls=%fused_computation | loop fusion | bytes 256 | tf_op jit(solution)/shard_map/squeeze | solution.py:542
  102.0 1.7 %copy.9 = f32[2,32,1280]{2,1,0:T(8,128)} copy(f32[2,32,1280]{2,1,0:T(8,128)} %bitcast.4) | data formatting | bytes 655360

commit v3 on v2

v3 whole, which is shorter than its diff:
```python
import functools
import math

import jax
import jax.numpy as jnp
from jax import lax
from jax.experimental import pallas as pl
from jax.experimental.pallas import tpu as pltpu
from jax.sharding import PartitionSpec as P

F32 = jnp.float32
BF16 = jnp.bfloat16
MESH = pl.DeviceIdType.MESH
LANES = 128
GROUP = 4
LOAD = 2
AHEAD = 2
UNROLL = 16
BEHIND = 1


def nn(lhs, rhs):
    return jnp.dot(lhs, rhs, preferred_element_type=F32)


def nt(lhs, rhs):
    return lax.dot_general(lhs, rhs, (((1,), (1,)), ((), ())), preferred_element_type=F32)


def lanes(*parts):
    return jnp.concatenate(parts, axis=1)


def stacked(*parts):
    return jnp.concatenate(parts, axis=0)


def times_factor(vec):
    half = vec.shape[0] // 2
    re, im = vec[:half], vec[half:]
    return stacked(lanes(re, -im), lanes(im, re))


def times_conj_factor(vec):
    half = vec.shape[0] // 2
    re, im = vec[:half], vec[half:]
    return stacked(lanes(re, im), lanes(im, -re))


def to_row(acc):
    pad = jnp.zeros((LANES - acc.shape[0], LANES), F32)
    return jnp.sum(stacked(acc, pad).T, axis=0, keepdims=True)


def to_col(row, sources):
    col = jnp.broadcast_to(row, (LANES, LANES)).T[:sources]
    return stacked(col, col)


def split3(row):
    high = row.astype(BF16).astype(F32)
    rest = row - high
    mid = rest.astype(BF16).astype(F32)
    low = rest - mid
    return stacked(high, mid, low, jnp.zeros((13, LANES), F32)).astype(BF16)


def kernel(
    dims,
    rhs,
    u_hbm,
    v_hbm,
    ranks,
    assign,
    out,
    phi_out,
    d_out,
    v_own,
    u_fac,
    v_fac,
    u_tr,
    v_tr,
    coeffs,
    d_full,
    x_send,
    x_recv,
    y_own,
    y_send,
    y_recv,
    z_acc,
    z_send,
    z_recv,
    v_full,
    gathered0,
    gathered1,
    picked,
    sib_recv,
    natural,
    cols,
    pair_send,
    pair_recv,
    row_send,
    row_recv,
    zrow_send,
    zrow_recv,
    fac_sem,
    send,
    recv,
    ag_r,
    fw_r,
    xs_r,
    zs_r,
    zg_r,
    ng_r,
    sib_r,
):
    chips, nx, ny, nz, tile_cols, sources = dims
    rows = 2 * sources
    zrows = rows // nz
    gathered = (gathered0, gathered1)
    me_c, me_z = lax.axis_index("col"), lax.axis_index("row")
    chip, core = lax.div(me_c, 2), lax.rem(me_c, 2)
    cx, cy = lax.div(chip, ny), lax.rem(chip, ny)
    sibling = chip * 2 + 1 - core

    def hops(q):
        return min(q // ny, nx - q // ny) + min(q % ny, ny - q % ny)

    near = sorted(range(chips), key=hops)
    far = near[::-1]

    def chip_to(q):
        return lax.rem(cx + lax.div(q, ny), nx) * ny + lax.rem(cy + lax.rem(q, ny), ny)

    def chip_from(q):
        return lax.rem(cx + nx - lax.div(q, ny), nx) * ny + lax.rem(cy + ny - lax.rem(q, ny), ny)

    def along_z(k):
        return lax.rem(me_z + k, nz)

    def remote(src, dst, send, recv, col, row):
        return pltpu.make_async_remote_copy(
            src_ref=src, dst_ref=dst, send_sem=send, recv_sem=recv,
            device_id=(col, row), device_id_type=MESH,
        )

    def copy_ag(rd, q):
        own = d_full.at[rd, chip, core]
        return remote(own, own, send.at[0], ag_r.at[q], chip_to(q) * 2 + core, me_z)

    def copy_fw(rd, q):
        here = d_full.at[rd, chip_from(q), core]
        return remote(here, here, send.at[1], fw_r.at[q], sibling, me_z)

    def copy_xs(rd, q):
        i = chip_to(q)
        return remote(
            x_send.at[rd, i], x_recv.at[rd, i], send.at[2], xs_r.at[q], sibling, me_z
        )

    def copy_ys(rd, q):
        i = chip_to(q)
        return remote(
            y_send.at[rd, i], y_recv.at[rd, q], send.at[3], recv.at[3], i * 2 + core, me_z
        )

    def copy_pair(rd):
        return remote(
            pair_send.at[rd], pair_recv.at[rd], send.at[4], recv.at[4], sibling, me_z
        )

    def copy_row(q):
        return remote(
            row_send, row_recv.at[q], send.at[5], recv.at[5], chip_to(q) * 2 + core, me_z
        )

    def copy_zrow(rd, k):
        return remote(
            zrow_send.at[rd], zrow_recv.at[rd, k], send.at[6], recv.at[6], me_c, along_z(k)
        )

    def copy_zs(rd, k, p):
        return remote(
            z_send.at[rd, along_z(k), p], z_recv.at[rd, k, p], send.at[7], zs_r.at[p], me_c,
            along_z(k),
        )

    def copy_zg(rd, k, p):
        own = v_full.at[rd, me_z, p]
        return remote(own, own, send.at[8], zg_r.at[p], me_c, along_z(k))

    def copy_ng(rd, q):
        own = gathered[rd].at[pl.ds(chip * tile_cols, tile_cols)]
        return remote(own, own, send.at[9 + 3 * rd], ng_r.at[rd], chip_to(q) * 2 + core, me_z)

    def copy_sib(rd):
        return remote(
            picked.at[rd, 1 - core], sib_recv.at[rd], send.at[10], sib_r.at[rd], sibling, me_z
        )

    def copy_nz(rd, k):
        own = natural.at[rd, me_z]
        return remote(own, own, send.at[11], recv.at[11], me_c, along_z(k))

    def arrived(ref, sem):
        remote(ref, ref, sem, sem, sibling, me_z).wait_recv()

    def has_left(ref, sem):
        remote(ref, ref, sem, sem, sibling, me_z).wait_send()

    def loop(low, high, body):
        lax.fori_loop(low, high, lambda i, c: (body(i), c)[1], 0)

    def factor_copies(g):
        some = pl.ds(g * LOAD, LOAD)
        return (
            pltpu.make_async_copy(v_hbm.at[some], v_fac.at[some], fac_sem.at[2 * g]),
            pltpu.make_async_copy(u_hbm.at[some], u_fac.at[some], fac_sem.at[2 * g + 1]),
        )

    lane = lax.broadcasted_iota(jnp.int32, (rows, LANES), 1)

    def masked(value, i, p):
        return jnp.where(lane < ranks[p, i], value, 0.0).astype(BF16)

    def lane_sums(square, acc):
        for at in range(0, square.shape[1], LANES):
            part = square[:, at : at + LANES]
            acc = acc + part[:sources] + part[sources:]
        return acc

    def transpose(fac, held, i):
        for p in range(tile_cols):
            for c in range(2):
                held[i, p, c * LANES : (c + 1) * LANES] = fac[i, p, c].T

    def start_factor(g):
        for copy in factor_copies(g):
            copy.start()

    loop(0, chips // LOAD, start_factor)
    d_full[0, chip, core] = rhs[...].astype(BF16)

    barrier = pltpu.get_barrier_semaphore()

    def greet(col, row):
        pl.semaphore_signal(barrier, inc=1, device_id=(col, row), device_id_type=MESH)

    greet(sibling, me_z)
    for k in range(1, nz):
        greet(me_c, along_z(k))
    loop(1, chips, lambda q: greet(chip_to(q) * 2 + core, me_z))
    pl.semaphore_wait(barrier, chips - 1 + 1 + nz - 1)

    def send_data(rd):
        copy_fw(rd, 0).start()
        for q in far[:-1]:
            copy_ag(rd, q).start()

    send_data(0)

    def ready(g):
        for copy in factor_copies(g):
            copy.wait()
        for i in range(LOAD):
            transpose(v_fac, v_tr, g * LOAD + i)

    loop(0, chips // LOAD, ready)

    def adjoint(rd):
        def pass_on(q):
            copy_ag(rd, q).wait_recv()
            copy_fw(rd, q).start()

        for q in near[1 : AHEAD * GROUP]:
            pass_on(q)

        acc = jnp.zeros((sources, LANES), F32)
        for g in range(chips // GROUP):
            for q in near[(g + AHEAD) * GROUP : (g + AHEAD + 1) * GROUP]:
                pass_on(q)
            for q in near[g * GROUP : (g + 1) * GROUP]:
                i = chip_from(q)
                copy_fw(rd, q).wait_recv()
                data = lanes(d_full[rd, i, 0], d_full[rd, i, 1])
                wide = data.astype(F32)
                acc = lane_sums(wide * wide, acc)
                left = times_conj_factor(data)
                right = lanes(*[u_fac[i, p].reshape(-1, LANES) for p in range(tile_cols)])
                raw = nn(left, right)
                for p in range(tile_cols):
                    coeff = masked(raw[:, p * LANES : (p + 1) * LANES], i, p)
                    coeffs[p, i] = times_conj_factor(coeff)
        zrow_start(rd, to_row(acc))
        if rd == 1:
            loop(1, chips, lambda q: copy_ng(0, q).start())

        def column(p):
            left = lanes(*[coeffs[p, i] for i in range(chips)])
            z = nn(left, stacked(*[v_tr[i, p] for i in range(chips)]))
            z_acc[p] = z
            for r in range(nz):
                z_send[rd, r, p] = z[r * zrows : (r + 1) * zrows].astype(BF16)
            for k in range(1, nz):
                copy_zs(rd, k, p).start()

        for p in range(tile_cols):
            column(p)

    def zrow_start(rd, row):
        zrow_send[rd] = row
        for k in range(1, nz):
            copy_zrow(rd, k).start()

    def zrow_sum(rd):
        total = zrow_send[rd]
        arrived(zrow_recv.at[rd, pl.ds(1, nz - 1)], recv.at[6])
        for k in range(1, nz):
            total = total + zrow_recv[rd, k]
        return total

    own_rows = pl.ds(pl.multiple_of(me_z * zrows, zrows), zrows)

    def own_col(slot):
        part = cols[slot, own_rows, :]
        return lanes(part, part)

    def model(rd, finish):
        for p in range(tile_cols):
            total = z_acc[p, own_rows, :]
            arrived(z_recv.at[rd, pl.ds(1, nz - 1), p], zs_r.at[p])
            for k in range(1, nz):
                total = total + z_recv[rd, k, p].astype(F32)
            v_hat = finish(total, p)
            v_own[rd, p] = v_hat
            v_b = v_hat.astype(BF16)
            v_full[rd, me_z, p] = v_b
            for k in range(1, nz):
                copy_zg(rd, k, p).start()
            gathered[rd][chip * tile_cols + p] = v_b
        if rd == 1:
            loop(1, chips, lambda q: copy_ng(1, q).start())

    def forward(rd):
        acc = jnp.zeros((sources, LANES), F32)
        for p in range(tile_cols):
            arrived(v_full.at[rd, pl.ds(0, nz - 1), p], zg_r.at[p])
            vec = stacked(*[v_full[rd, r, p] for r in range(nz)])
            wide = vec.astype(F32)
            acc = lane_sums(wide * wide, acc)
            left = times_factor(vec)

            def group(g, left=left, p=p):
                some = min(UNROLL, chips)
                for h in range(some // 2):
                    where = [g * some + h * 2 + j for j in range(2)]
                    right = lanes(*[v_fac[i, p].reshape(-1, LANES) for i in where])
                    raw = nn(left, right)
                    for j, i in enumerate(where):
                        coeff = masked(raw[:, j * LANES : (j + 1) * LANES], i, p)
                        coeffs[p, i] = times_factor(coeff)

            loop(0, chips // min(UNROLL, chips), group)
        own = to_row(acc)
        pair_send[rd] = own
        copy_pair(rd).start()

        def compute(g):
            for q in far[g * GROUP : (g + 1) * GROUP]:
                i = chip_to(q)
                left = lanes(*[coeffs[p, i] for p in range(tile_cols)])
                y = nn(left, stacked(*[u_tr[i, p] for p in range(tile_cols)]))
                zero, one = y[:, :LANES], y[:, LANES:]
                y_own[i] = jnp.where(core == 0, zero, one)
                x_send[rd, i] = jnp.where(core == 0, one, zero).astype(BF16)
                copy_xs(rd, q).start()

        def finish(g, block):
            for q in far[g * GROUP : (g + 1) * GROUP]:
                i = chip_to(q)
                copy_xs(rd, q).wait_recv()
                y_send[rd, i, :rows] = (y_own[i] + x_recv[rd, i].astype(F32)).astype(BF16)
                y_send[rd, i, rows:] = block

                if q > 0:
                    copy_ys(rd, q).start()

        behind = min(BEHIND, chips // GROUP)
        for g in range(behind):
            compute(g)
        copy_pair(rd).wait_recv()
        block = split3(own + pair_recv[rd])

        for g in range(behind, chips // GROUP):
            compute(g)
            finish(g - behind, block)
        for g in range(chips // GROUP - behind, chips // GROUP):
            finish(g, block)

    def data_sum(rd):
        total = y_send[rd, chip].astype(F32)
        arrived(y_recv.at[rd, pl.ds(1, chips - 1)], recv.at[3])
        for q in range(1, chips):
            total = total + y_recv[rd, q].astype(F32)
        row = total[rows : rows + 1] + total[rows + 1 : rows + 2] + total[rows + 2 : rows + 3]
        return total[:rows], row

    def pick(rd, held):
        arrived(gathered[rd].at[pl.ds(0, (chips - 1) * tile_cols)], ng_r.at[rd])
        for j, (found, at) in enumerate(held):
            seg = gathered[rd][at].astype(F32) * found.astype(F32)
            picked[rd, j // tile_cols, j % tile_cols] = seg.astype(BF16)
        copy_sib(rd).start()

    def join(rd):
        copy_sib(rd).wait_recv()
        mine = picked[rd, core].astype(F32) + sib_recv[rd].astype(F32)
        natural[rd, me_z] = mine.astype(BF16)
        for k in range(1, nz):
            copy_nz(rd, k).start()

    def find_held():
        first = chip * (2 * tile_cols)
        zero = jnp.int32(0)

        def step(a, carry):
            found, at = list(carry[0]), list(carry[1])
            for t in range(tile_cols):
                held = assign[a * (2 * tile_cols) + core * tile_cols + t] - first
                for j in range(2 * tile_cols):
                    hit = held == j
                    found[j] = jnp.where(hit, 1, found[j])
                    at[j] = jnp.where(hit, a * tile_cols + t, at[j])
            return tuple(found), tuple(at)

        many = 2 * tile_cols
        found, at = lax.fori_loop(0, chips, step, ((zero,) * many, (zero,) * many))
        return list(zip(found, at))

    adjoint(0)
    def transpose_some(g):
        for i in range(4):
            transpose(u_fac, u_tr, g * 4 + i)

    loop(0, chips // 4, transpose_some)
    beta0 = jnp.sqrt(zrow_sum(0))
    cols[0] = to_col(beta0, sources)
    by_beta = own_col(0)
    model(0, lambda total, p: total / by_beta)

    forward(0)
    held = find_held()
    y, alpha0 = data_sum(0)
    alpha0 = jnp.sqrt(alpha0)
    cols[1] = to_col(alpha0, sources)
    d_hat = y / cols[1] - cols[1] * (rhs[...] / cols[0])
    d_full[1, chip, core] = d_hat.astype(BF16)
    send_data(1)
    d_out[...] = d_hat
    adjoint(1)
    beta1 = jnp.sqrt(zrow_sum(1))
    cols[2] = to_col(beta1, sources)
    beta, alpha = own_col(2), own_col(1)
    model(1, lambda total, p: total / beta - beta * (v_own[0, p] / alpha))

    pick(0, held)
    forward(1)
    join(0)
    pick(1, held)
    y, alpha1 = data_sum(1)
    alpha1 = jnp.sqrt(alpha1)
    cols[3] = to_col(alpha1, sources)
    d_hat = y / cols[3] - cols[3] * (d_out[...] / cols[2])
    square = d_hat * d_hat
    own = to_row(square[:sources] + square[sources:])
    pair_send[2] = own
    copy_pair(2).start()
    d_out[...] = d_hat
    join(1)
    copy_pair(2).wait_recv()
    row_send[...] = own + pair_recv[2]
    loop(1, chips, lambda q: copy_row(q).start())
    rho1 = jnp.sqrt(alpha0 * alpha0 + beta1 * beta1)
    cosine = alpha0 / rho1
    sine = beta1 / rho1
    theta = sine * alpha1
    rhobar = -cosine * alpha1
    phi1 = cosine * beta0
    phibar = sine * beta0
    total = row_send[...]
    arrived(row_recv.at[pl.ds(1, chips - 1)], recv.at[5])
    for q in range(1, chips):
        total = total + row_recv[q]
    zrow_start(2, total)
    arrived(natural.at[:, pl.ds(0, nz - 1)], recv.at[11])
    beta2 = jnp.sqrt(zrow_sum(2))
    rho2 = jnp.sqrt(rhobar * rhobar + beta2 * beta2)
    cosine = rhobar / rho2
    sine = beta2 / rho2
    step2 = cosine * phibar / rho2
    phi_out[0:1] = sine * phibar
    phi_out[1:2] = sine / rho2
    phi_out[2:3] = theta / rho1
    phi_out[3:4] = alpha0
    phi_out[4:5] = alpha1
    first = to_col((phi1 / rho1 - step2 * (theta / rho1)) / alpha0, sources)
    second = to_col(step2 / alpha1, sources)
    width = natural.shape[-1]
    for p in range(tile_cols):
        for at in range(0, width, LANES):
            one = stacked(*[natural[0, r, p, :, at : at + LANES] for r in range(nz)])
            two = stacked(*[natural[1, r, p, :, at : at + LANES] for r in range(nz)])
            out[:, p * width + at : p * width + at + LANES] = (
                first * one.astype(F32) + second * two.astype(F32)
            )

    others, zs = pl.ds(1, chips - 1), pl.ds(1, nz - 1)
    has_left(d_full.at[:, others, 0], send.at[0])
    has_left(d_full.at[:, :, 0], send.at[1])
    has_left(x_send, send.at[2])
    has_left(y_send.at[:, others], send.at[3])
    has_left(pair_send, send.at[4])
    has_left(row_recv.at[others], send.at[5])
    has_left(zrow_recv.at[:, zs], send.at[6])
    has_left(z_send.at[:, zs], send.at[7])
    has_left(v_full.at[:, zs], send.at[8])
    for rd in range(2):
        has_left(gathered[rd].at[pl.ds(0, (chips - 1) * tile_cols)], send.at[9 + 3 * rd])
    has_left(picked.at[0], send.at[10])
    has_left(natural.at[:, zs], send.at[11])


def last_adjoint(d_hat, v_hats, scalars, u_factor, v_factor, ranks):
    tile_rows, tile_cols, _, tile_size, rank_cap = u_factor.shape
    sources = d_hat.shape[0] // 2
    rank_iota = lax.broadcasted_iota(jnp.int32, (tile_rows, tile_cols, 1, 1, rank_cap), 4)
    mask = (rank_iota < ranks[:, :, None, None, None]).astype(F32)
    d_hat = d_hat.reshape(2, sources, -1)
    beta = jnp.sqrt(lax.psum(jnp.sum(d_hat * d_hat, axis=(0, 2)), ("col", "row")))
    data = lax.all_gather(d_hat.astype(BF16), "col", axis=2, tiled=True)
    data = data.reshape(2, sources, tile_rows, tile_size)
    raw = jnp.einsum("ipcnk,dsin->ipcdsk", u_factor, data, preferred_element_type=F32)
    coeff = jnp.stack([raw[:, :, 0, 0] + raw[:, :, 1, 1], raw[:, :, 0, 1] - raw[:, :, 1, 0]], axis=2)
    coeff = (coeff * mask).astype(BF16)
    prod = jnp.einsum("ipcnk,ipdsk->cdspn", v_factor, coeff, preferred_element_type=F32)
    model = jnp.stack([prod[0, 0] + prod[1, 1], prod[0, 1] - prod[1, 0]], axis=0)
    model = lax.psum(model, "row").reshape(2, sources, tile_cols * tile_size)
    sine_by_rho, theta_by_rho, alpha0, alpha1 = [row[None, :, None] for row in scalars]
    v_hats = lax.all_gather(v_hats, "row", axis=2, tiled=True)
    v_hats = v_hats.transpose(0, 2, 1, 3).reshape(2, *model.shape)
    v_prev = v_hats[1] / alpha1
    w_prev = v_prev - theta_by_rho * (v_hats[0] / alpha0)
    v_hat = model / beta[None, :, None] - beta[None, :, None] * v_prev
    alpha = jnp.sqrt(lax.psum(jnp.sum(v_hat * v_hat, axis=(0, 2)), "col"))
    v_vec = v_hat / alpha[None, :, None]
    return v_vec, alpha, v_vec - sine_by_rho * alpha[None, :, None] * w_prev


def on_device(nz, rhs, u_factor, v_factor, ranks, assign):
    tile_rows, tile_cols, _, tile_size, _ = u_factor.shape
    sources = rhs.shape[1]
    rows = 2 * sources
    zrows = rows // nz
    chips = tile_rows
    ny = math.isqrt(chips)
    nx = chips // ny
    dims = (chips, nx, ny, nz, tile_cols, sources)
    seg = (tile_cols, zrows, tile_size)
    dma = pltpu.SemaphoreType.DMA
    vmem = pl.BlockSpec(memory_space=pltpu.VMEM)
    smem = pl.BlockSpec(memory_space=pltpu.SMEM)
    hbm = pl.BlockSpec(memory_space=pl.ANY)
    out, scalars, d_hat, v_hats = pl.pallas_call(
        functools.partial(kernel, dims),
        out_shape=[
            jax.ShapeDtypeStruct((rows, tile_cols * tile_size), F32),
            jax.ShapeDtypeStruct((5, LANES), F32),
            jax.ShapeDtypeStruct((rows, LANES), F32),
            jax.ShapeDtypeStruct((2, *seg), F32),
        ],
        in_specs=[vmem, hbm, hbm, smem, smem],
        out_specs=[vmem] * 4,
        scratch_shapes=[
            pltpu.VMEM(u_factor.shape, BF16),
            pltpu.VMEM(v_factor.shape, BF16),
            pltpu.VMEM((chips, tile_cols, 2 * LANES, tile_size), BF16),
            pltpu.VMEM((chips, tile_cols, 2 * LANES, tile_size), BF16),
            pltpu.VMEM((tile_cols, chips, rows, 2 * LANES), BF16),
            pltpu.VMEM((2, chips, 2, rows, LANES), BF16),
            pltpu.VMEM((2, chips, rows, LANES), BF16),
            pltpu.VMEM((2, chips, rows, LANES), BF16),
            pltpu.VMEM((chips, rows, LANES), F32),
            pltpu.VMEM((2, chips, rows + 16, LANES), BF16),
            pltpu.VMEM((2, chips, rows + 16, LANES), BF16),
            pltpu.VMEM((tile_cols, rows, tile_size), F32),
            pltpu.VMEM((2, nz, *seg), BF16),
            pltpu.VMEM((2, nz, *seg), BF16),
            pltpu.VMEM((2, nz, *seg), BF16),
            pltpu.VMEM((chips * tile_cols, zrows, tile_size), BF16),
            pltpu.VMEM((chips * tile_cols, zrows, tile_size), BF16),
            pltpu.VMEM((2, 2, *seg), BF16),
            pltpu.VMEM((2, *seg), BF16),
            pltpu.VMEM((2, nz, *seg), BF16),
            pltpu.VMEM((4, rows, LANES), F32),
            pltpu.VMEM((3, 1, LANES), F32),
            pltpu.VMEM((3, 1, LANES), F32),
            pltpu.VMEM((1, LANES), F32),
            pltpu.VMEM((chips, 1, LANES), F32),
            pltpu.VMEM((3, 1, LANES), F32),
            pltpu.VMEM((3, nz, 1, LANES), F32),
            dma((chips,)),
            dma((13,)), dma((12,)),
            dma((chips,)), dma((chips,)), dma((chips,)),
            dma((tile_cols,)), dma((tile_cols,)),
            dma((2,)), dma((2,)),
        ],
        compiler_params=pltpu.CompilerParams(
            collective_id=0, has_side_effects=True, vmem_limit_bytes=60 * 2**20
        ),
        name="lsqr",
    )(rhs.reshape(rows, LANES), u_factor, v_factor, ranks.T, assign)
    last_adjoint(d_hat, v_hats, scalars[1:, :sources], u_factor, v_factor, ranks)
    phibar = scalars[0, :sources]
    return out.reshape(2, sources, tile_cols * tile_size), phibar


def solution(mesh):
    return jax.shard_map(
        functools.partial(on_device, mesh.shape["row"]),
        mesh=mesh,
        in_specs=(
            P(None, None, "row", "col"),
            P("row", "col", None, None, None),
            P("row", "col", None, None, None),
            P("row", "col"),
            P(),
        ),
        out_specs=(P(None, None, "col"), P()),
        check_vma=False,
    )
```

time: 104 us -> 87.9 us (0.85)
  Pallas kernels: 98.8 us -> 84.1 us
  local copies, waits for them, and re-layouts: 4.26 us -> 2.9 us
    pallas_call x1, Pallas kernels: 98.8 us -> 84.1 us  [on_device(): pl.pallas_call(functools.partial(kernel, dims), out_shape=[jax.ShapeDtype...]
    unnamed x2 -> x1, local copies, waits for them, and re-layouts: 3.08 us -> 1.72 us
where the time goes in v3:
time: 87.9 us; the launch traced here: 87.7 us
  Pallas kernels  84.1 us (96%)
  local copies, waits for them, and re-layouts  2.9 us (3%)
    pallas_call x1, Pallas kernels, on_device(): pl.pallas_call(functools.partial(kernel, dims), out_shape=[jax.ShapeDtype...  84.1 us

profile of v3, /device:TPU:0, one launch (start us, length us, event | category | flops | bytes accessed | tf_op | source)
XLA Modules:
  0.0 87.7 jit_solution(18242513123023724348)
XLA Ops:
  0.6 84.1 %lsqr.1 = (f32[64,1280]{1,0:T(8,128)}, f32[5,128]{1,0:T(8,128)}, f32[64,128]{1,0:T(8,128)}, f32[2,5,16,256]{3,2,1,0:T(8,128)}) custom-call(f32[64,128]{1,0:T(8,128)} %bitcast.6, bf16[16,5,2,256,128]{4,3,2,1,0:T(8,128)(2,1)} %u_hbm.1, bf16[16,5,2,256,128]{4,3,2,1,0:T(8,128)(2,1)} %v_hbm.1, s32[5,16]{1,0:T(8,128)} %bitcast.7, s32[160]{0:T(256)} %assign.1), custom_call_target="tpu_custom_call" | custom-call | tf_op jit(solution)/shard_map/lsqr/pallas_call | solution.py:573
  84.8 1.2 %slice_bitcast_fusion = f32[32]{0:T(128)} fusion(f32[5,128]{1,0:T(8,128)} %get-tuple-element.5), kind=kLoop, calls=%fused_computation | loop fusion | bytes 256 | tf_op jit(solution)/shard_map/squeeze | solution.py:623
  85.9 1.7 %copy.8 = f32[2,32,1280]{2,1,0:T(8,128)} copy(f32[2,32,1280]{2,1,0:T(8,128)} %bitcast.5) | data formatting | bytes 655360

commit v4 on v3

--- a/solution.py
+++ b/solution.py
@@ -12,11 +12,11 @@
 BF16 = jnp.bfloat16
 MESH = pl.DeviceIdType.MESH
 LANES = 128
-GROUP = 4
+GROUP = 2
 LOAD = 2
 AHEAD = 2
 UNROLL = 16
-BEHIND = 1
+BEHIND = 2
 
 
 def nn(lhs, rhs):
@@ -72,7 +72,7 @@
     v_hbm,
     ranks,
     assign,
-    out,
+    nat_out,
     phi_out,
     d_out,
     v_own,
@@ -103,6 +103,8 @@
     row_recv,
     zrow_send,
     zrow_recv,
+    last_send,
+    last_recv,
     fac_sem,
     send,
     recv,
@@ -179,6 +181,12 @@
             zrow_send.at[rd], zrow_recv.at[rd, k], send.at[6], recv.at[6], me_c, along_z(k)
         )
 
+    def beside(m):
+        return chip * 2 + lax.rem(core + m % 2, 2), along_z(m // 2)
+
+    def copy_last(m):
+        return remote(last_send, last_recv.at[m], send.at[13], recv.at[12], *beside(m))
+
     def copy_zs(rd, k, p):
         return remote(
             z_send.at[rd, along_z(k), p], z_recv.at[rd, k, p], send.at[7], zs_r.at[p], me_c,
@@ -246,11 +254,10 @@
     def greet(col, row):
         pl.semaphore_signal(barrier, inc=1, device_id=(col, row), device_id_type=MESH)
 
-    greet(sibling, me_z)
-    for k in range(1, nz):
-        greet(me_c, along_z(k))
+    for m in range(1, 2 * nz):
+        greet(*beside(m))
     loop(1, chips, lambda q: greet(chip_to(q) * 2 + core, me_z))
-    pl.semaphore_wait(barrier, chips - 1 + 1 + nz - 1)
+    pl.semaphore_wait(barrier, chips - 1 + 2 * nz - 1)
 
     def send_data(rd):
         copy_fw(rd, 0).start()
@@ -291,21 +298,21 @@
                 for p in range(tile_cols):
                     coeff = masked(raw[:, p * LANES : (p + 1) * LANES], i, p)
                     coeffs[p, i] = times_conj_factor(coeff)
-        zrow_start(rd, to_row(acc))
-        if rd == 1:
-            loop(1, chips, lambda q: copy_ng(0, q).start())
-
-        def column(p):
-            left = lanes(*[coeffs[p, i] for i in range(chips)])
-            z = nn(left, stacked(*[v_tr[i, p] for i in range(chips)]))
-            z_acc[p] = z
-            for r in range(nz):
-                z_send[rd, r, p] = z[r * zrows : (r + 1) * zrows].astype(BF16)
-            for k in range(1, nz):
-                copy_zs(rd, k, p).start()
-
-        for p in range(tile_cols):
-            column(p)
+            some = [chip_from(q) for q in near[g * GROUP : (g + 1) * GROUP]]
+            last = g == chips // GROUP - 1
+            if last:
+                zrow_start(rd, to_row(acc))
+            for p in range(tile_cols):
+                left = lanes(*[coeffs[p, i] for i in some])
+                z = nn(left, stacked(*[v_tr[i, p] for i in some]))
+                if g > 0:
+                    z += z_acc[p]
+                z_acc[p] = z
+                if last:
+                    for r in range(nz):
+                        z_send[rd, r, p] = z[r * zrows : (r + 1) * zrows].astype(BF16)
+                    for k in range(1, nz):
+                        copy_zs(rd, k, p).start()
 
     def zrow_start(rd, row):
         zrow_send[rd] = row
@@ -338,8 +345,7 @@
             for k in range(1, nz):
                 copy_zg(rd, k, p).start()
             gathered[rd][chip * tile_cols + p] = v_b
-        if rd == 1:
-            loop(1, chips, lambda q: copy_ng(1, q).start())
+        loop(1, chips, lambda q: copy_ng(rd, q).start())
 
     def forward(rd):
         acc = jnp.zeros((sources, LANES), F32)
@@ -473,13 +479,11 @@
     d_hat = y / cols[3] - cols[3] * (d_out[...] / cols[2])
     square = d_hat * d_hat
     own = to_row(square[:sources] + square[sources:])
-    pair_send[2] = own
-    copy_pair(2).start()
+    row_send[...] = own
+    for q in far[:-1]:
+        copy_row(q).start()
     d_out[...] = d_hat
     join(1)
-    copy_pair(2).wait_recv()
-    row_send[...] = own + pair_recv[2]
-    loop(1, chips, lambda q: copy_row(q).start())
     rho1 = jnp.sqrt(alpha0 * alpha0 + beta1 * beta1)
     cosine = alpha0 / rho1
     sine = beta1 / rho1
@@ -491,28 +495,27 @@
     arrived(row_recv.at[pl.ds(1, chips - 1)], recv.at[5])
     for q in range(1, chips):
         total = total + row_recv[q]
-    zrow_start(2, total)
+    last_send[...] = total
+    for m in range(1, 2 * nz):
+        copy_last(m).start()
     arrived(natural.at[:, pl.ds(0, nz - 1)], recv.at[11])
-    beta2 = jnp.sqrt(zrow_sum(2))
+    nat_out[...] = natural[...]
+    arrived(last_recv.at[pl.ds(1, 2 * nz - 1)], recv.at[12])
+    for m in range(1, 2 * nz):
+        total = total + last_recv[m]
+    beta2 = jnp.sqrt(total)
     rho2 = jnp.sqrt(rhobar * rhobar + beta2 * beta2)
     cosine = rhobar / rho2
     sine = beta2 / rho2
     step2 = cosine * phibar / rho2
+    phi_out[...] = jnp.zeros_like(phi_out)
     phi_out[0:1] = sine * phibar
     phi_out[1:2] = sine / rho2
     phi_out[2:3] = theta / rho1
     phi_out[3:4] = alpha0
     phi_out[4:5] = alpha1
-    first = to_col((phi1 / rho1 - step2 * (theta / rho1)) / alpha0, sources)
-    second = to_col(step2 / alpha1, sources)
-    width = natural.shape[-1]
-    for p in range(tile_cols):
-        for at in range(0, width, LANES):
-            one = stacked(*[natural[0, r, p, :, at : at + LANES] for r in range(nz)])
-            two = stacked(*[natural[1, r, p, :, at : at + LANES] for r in range(nz)])
-            out[:, p * width + at : p * width + at + LANES] = (
-                first * one.astype(F32) + second * two.astype(F32)
-            )
+    phi_out[5:6] = (phi1 / rho1 - step2 * (theta / rho1)) / alpha0
+    phi_out[6:7] = step2 / alpha1
 
     others, zs = pl.ds(1, chips - 1), pl.ds(1, nz - 1)
     has_left(d_full.at[:, others, 0], send.at[0])
@@ -528,6 +531,21 @@
         has_left(gathered[rd].at[pl.ds(0, (chips - 1) * tile_cols)], send.at[9 + 3 * rd])
     has_left(picked.at[0], send.at[10])
     has_left(natural.at[:, zs], send.at[11])
+    has_left(last_recv.at[pl.ds(1, 2 * nz - 1)], send.at[13])
+
+
+def combine(nz, scalars, natural, out, phi):
+    sources = phi.shape[1]
+    _, _, tile_cols, _, width = natural.shape
+    first, second = to_col(scalars[5:6], sources), to_col(scalars[6:7], sources)
+    phi[...] = scalars[0:1, :sources]
+    for p in range(tile_cols):
+        for at in range(0, width, LANES):
+            one = stacked(*[natural[0, r, p, :, at : at + LANES] for r in range(nz)])
+            two = stacked(*[natural[1, r, p, :, at : at + LANES] for r in range(nz)])
+            out[:, p * width + at : p * width + at + LANES] = (
+                first * one.astype(F32) + second * two.astype(F32)
+            )
 
 
 def last_adjoint(d_hat, v_hats, scalars, u_factor, v_factor, ranks):
@@ -570,11 +588,11 @@
     vmem = pl.BlockSpec(memory_space=pltpu.VMEM)
     smem = pl.BlockSpec(memory_space=pltpu.SMEM)
     hbm = pl.BlockSpec(memory_space=pl.ANY)
-    out, scalars, d_hat, v_hats = pl.pallas_call(
+    natural, scalars, d_hat, v_hats = pl.pallas_call(
         functools.partial(kernel, dims),
         out_shape=[
-            jax.ShapeDtypeStruct((rows, tile_cols * tile_size), F32),
-            jax.ShapeDtypeStruct((5, LANES), F32),
+            jax.ShapeDtypeStruct((2, nz, *seg), BF16),
+            jax.ShapeDtypeStruct((8, LANES), F32),
             jax.ShapeDtypeStruct((rows, LANES), F32),
             jax.ShapeDtypeStruct((2, *seg), F32),
         ],
@@ -602,14 +620,16 @@
             pltpu.VMEM((2, *seg), BF16),
             pltpu.VMEM((2, nz, *seg), BF16),
             pltpu.VMEM((4, rows, LANES), F32),
-            pltpu.VMEM((3, 1, LANES), F32),
-            pltpu.VMEM((3, 1, LANES), F32),
+            pltpu.VMEM((2, 1, LANES), F32),
+            pltpu.VMEM((2, 1, LANES), F32),
             pltpu.VMEM((1, LANES), F32),
             pltpu.VMEM((chips, 1, LANES), F32),
-            pltpu.VMEM((3, 1, LANES), F32),
-            pltpu.VMEM((3, nz, 1, LANES), F32),
+            pltpu.VMEM((2, 1, LANES), F32),
+            pltpu.VMEM((2, nz, 1, LANES), F32),
+            pltpu.VMEM((1, LANES), F32),
+            pltpu.VMEM((2 * nz, 1, LANES), F32),
             dma((chips,)),
-            dma((13,)), dma((12,)),
+            dma((14,)), dma((13,)),
             dma((chips,)), dma((chips,)), dma((chips,)),
             dma((tile_cols,)), dma((tile_cols,)),
             dma((2,)), dma((2,)),
@@ -619,9 +639,18 @@
         ),
         name="lsqr",
     )(rhs.reshape(rows, LANES), u_factor, v_factor, ranks.T, assign)
-    last_adjoint(d_hat, v_hats, scalars[1:, :sources], u_factor, v_factor, ranks)
-    phibar = scalars[0, :sources]
-    return out.reshape(2, sources, tile_cols * tile_size), phibar
+    last_adjoint(d_hat, v_hats, scalars[1:5, :sources], u_factor, v_factor, ranks)
+    out, phibar = pl.pallas_call(
+        functools.partial(combine, nz),
+        out_shape=[
+            jax.ShapeDtypeStruct((rows, tile_cols * tile_size), F32),
+            jax.ShapeDtypeStruct((1, sources), F32),
+        ],
+        in_specs=[vmem] * 2,
+        out_specs=[vmem] * 2,
+        name="combine",
+    )(scalars, natural)
+    return out.reshape(2, sources, tile_cols * tile_size), phibar.reshape(sources)
 
 
 def solution(mesh):

time: 87.9 us -> 83.4 us (0.949)
  local copies, waits for them, and re-layouts: 2.9 us -> 0 us
  Pallas kernels: 84.1 us -> 81.8 us
    pallas_call x1, Pallas kernels: 84.1 us -> 80 us  [on_device(): pl.pallas_call(functools.partial(kernel, dims), out_shape=[jax.ShapeDtype...]
    pallas_call x0 -> x1, Pallas kernels: none -> 1.83 us  [on_device(): pl.pallas_call(functools.partial(combine, nz), out_shape=[jax.ShapeDtypeS...]
    unnamed x1 -> x0, local copies, waits for them, and re-layouts: 1.72 us -> none
    squeeze x1 -> x0, local copies, waits for them, and re-layouts: 1.19 us -> none  [on_device(): phibar = scalars[0, :sources]]
where the time goes in v4:
time: 83.4 us; the launch traced here: 82.5 us
  Pallas kernels  81.8 us (98%)
    pallas_call x1, Pallas kernels, on_device(): pl.pallas_call(functools.partial(kernel, dims), out_shape=[jax.ShapeDtype...  80 us
    pallas_call x1, Pallas kernels, on_device(): pl.pallas_call(functools.partial(combine, nz), out_shape=[jax.ShapeDtypeS...  1.83 us

profile of v4, /device:TPU:0, one launch (start us, length us, event | category | flops | bytes accessed | tf_op | source)
XLA Modules:
  0.0 82.5 jit_solution(1020482936883754306)
XLA Ops:
  0.6 80.0 %lsqr.1 = (bf16[2,4,5,16,256]{4,3,2,1,0:T(8,128)(2,1)}, f32[8,128]{1,0:T(8,128)}, f32[64,128]{1,0:T(8,128)}, f32[2,5,16,256]{3,2,1,0:T(8,128)}) custom-call(f32[64,128]{1,0:T(8,128)} %bitcast.4, bf16[16,5,2,256,128]{4,3,2,1,0:T(8,128)(2,1)} %u_hbm.1, bf16[16,5,2,256,128]{4,3,2,1,0:T(8,128)(2,1)} %v_hbm.1, s32[5,16]{1,0:T(8,128)} %bitcast.5, s32[160]{0:T(256)} %assign.1), custom_call_target="tpu_custom_call" | custom-call | tf_op jit(solution)/shard_map/lsqr/pallas_call | solution.py:591
  80.6 1.8 %combine.1 = (f32[64,1280]{1,0:T(8,128)}, f32[1,32]{1,0:T(1,128)}) custom-call(f32[8,128]{1,0:T(8,128)} %get-tuple-element.6.scalars, bf16[2,4,5,16,256]{4,3,2,1,0:T(8,128)(2,1)} %get-tuple-element.7.natural), custom_call_target="tpu_custom_call" | custom-call | tf_op jit(solution)/shard_map/combine/pallas_call | solution.py:643

commit v5 on v4

--- a/solution.py
+++ b/solution.py
@@ -55,14 +55,6 @@
 def to_col(row, sources):
     col = jnp.broadcast_to(row, (LANES, LANES)).T[:sources]
     return stacked(col, col)
-
-
-def split3(row):
-    high = row.astype(BF16).astype(F32)
-    rest = row - high
-    mid = rest.astype(BF16).astype(F32)
-    low = rest - mid
-    return stacked(high, mid, low, jnp.zeros((13, LANES), F32)).astype(BF16)
 
 
 def kernel(
@@ -128,6 +120,7 @@
     def hops(q):
         return min(q // ny, nx - q // ny) + min(q % ny, ny - q % ny)
 
+    z_order = sorted(range(1, nz), key=lambda k: -min(k, nz - k))
     near = sorted(range(chips), key=hops)
     far = near[::-1]
 
@@ -171,9 +164,10 @@
             pair_send.at[rd], pair_recv.at[rd], send.at[4], recv.at[4], sibling, me_z
         )
 
-    def copy_row(q):
+    def copy_row(rd, q):
         return remote(
-            row_send, row_recv.at[q], send.at[5], recv.at[5], chip_to(q) * 2 + core, me_z
+            row_send.at[rd], row_recv.at[rd, q], send.at[5], recv.at[13 if rd == 2 else 5],
+            chip_to(q) * 2 + core, me_z,
         )
 
     def copy_zrow(rd, k):
@@ -242,6 +236,14 @@
             for c in range(2):
                 held[i, p, c * LANES : (c + 1) * LANES] = fac[i, p, c].T
 
+    barrier = pltpu.get_barrier_semaphore()
+
+    def greet(col, row):
+        pl.semaphore_signal(barrier, inc=1, device_id=(col, row), device_id_type=MESH)
+
+    for m in range(1, 2 * nz):
+        greet(*beside(m))
+    loop(1, chips, lambda q: greet(chip_to(q) * 2 + core, me_z))
     def start_factor(g):
         for copy in factor_copies(g):
             copy.start()
@@ -249,14 +251,6 @@
     loop(0, chips // LOAD, start_factor)
     d_full[0, chip, core] = rhs[...].astype(BF16)
 
-    barrier = pltpu.get_barrier_semaphore()
-
-    def greet(col, row):
-        pl.semaphore_signal(barrier, inc=1, device_id=(col, row), device_id_type=MESH)
-
-    for m in range(1, 2 * nz):
-        greet(*beside(m))
-    loop(1, chips, lambda q: greet(chip_to(q) * 2 + core, me_z))
     pl.semaphore_wait(barrier, chips - 1 + 2 * nz - 1)
 
     def send_data(rd):
@@ -311,7 +305,7 @@
                 if last:
                     for r in range(nz):
                         z_send[rd, r, p] = z[r * zrows : (r + 1) * zrows].astype(BF16)
-                    for k in range(1, nz):
+                    for k in z_order:
                         copy_zs(rd, k, p).start()
 
     def zrow_start(rd, row):
@@ -342,7 +336,7 @@
             v_own[rd, p] = v_hat
             v_b = v_hat.astype(BF16)
             v_full[rd, me_z, p] = v_b
-            for k in range(1, nz):
+            for k in z_order:
                 copy_zg(rd, k, p).start()
             gathered[rd][chip * tile_cols + p] = v_b
         loop(1, chips, lambda q: copy_ng(rd, q).start())
@@ -381,12 +375,11 @@
                 x_send[rd, i] = jnp.where(core == 0, one, zero).astype(BF16)
                 copy_xs(rd, q).start()
 
-        def finish(g, block):
+        def finish(g):
             for q in far[g * GROUP : (g + 1) * GROUP]:
                 i = chip_to(q)
                 copy_xs(rd, q).wait_recv()
-                y_send[rd, i, :rows] = (y_own[i] + x_recv[rd, i].astype(F32)).astype(BF16)
-                y_send[rd, i, rows:] = block
+                y_send[rd, i] = (y_own[i] + x_recv[rd, i].astype(F32)).astype(BF16)
 
                 if q > 0:
                     copy_ys(rd, q).start()
@@ -395,21 +388,29 @@
         for g in range(behind):
             compute(g)
         copy_pair(rd).wait_recv()
-        block = split3(own + pair_recv[rd])
+        row_send[rd] = own + pair_recv[rd]
+        for q in far[:-1]:
+            copy_row(rd, q).start()
 
         for g in range(behind, chips // GROUP):
             compute(g)
-            finish(g - behind, block)
+            finish(g - behind)
         for g in range(chips // GROUP - behind, chips // GROUP):
-            finish(g, block)
+            finish(g)
 
     def data_sum(rd):
         total = y_send[rd, chip].astype(F32)
         arrived(y_recv.at[rd, pl.ds(1, chips - 1)], recv.at[3])
         for q in range(1, chips):
             total = total + y_recv[rd, q].astype(F32)
-        row = total[rows : rows + 1] + total[rows + 1 : rows + 2] + total[rows + 2 : rows + 3]
-        return total[:rows], row
+        return total
+
+    def row_sum(rd):
+        total = row_send[rd]
+        arrived(row_recv.at[rd, pl.ds(1, chips - 1)], recv.at[13 if rd == 2 else 5])
+        for q in range(1, chips):
+            total = total + row_recv[rd, q]
+        return total
 
     def pick(rd, held):
         arrived(gathered[rd].at[pl.ds(0, (chips - 1) * tile_cols)], ng_r.at[rd])
@@ -456,9 +457,9 @@
 
     forward(0)
     held = find_held()
-    y, alpha0 = data_sum(0)
-    alpha0 = jnp.sqrt(alpha0)
+    alpha0 = jnp.sqrt(row_sum(0))
     cols[1] = to_col(alpha0, sources)
+    y = data_sum(0)
     d_hat = y / cols[1] - cols[1] * (rhs[...] / cols[0])
     d_full[1, chip, core] = d_hat.astype(BF16)
     send_data(1)
@@ -471,17 +472,17 @@
 
     pick(0, held)
     forward(1)
-    join(0)
-    pick(1, held)
-    y, alpha1 = data_sum(1)
-    alpha1 = jnp.sqrt(alpha1)
+    alpha1 = jnp.sqrt(row_sum(1))
     cols[3] = to_col(alpha1, sources)
+    y = data_sum(1)
     d_hat = y / cols[3] - cols[3] * (d_out[...] / cols[2])
     square = d_hat * d_hat
     own = to_row(square[:sources] + square[sources:])
-    row_send[...] = own
+    row_send[2] = own
     for q in far[:-1]:
-        copy_row(q).start()
+        copy_row(2, q).start()
+    join(0)
+    pick(1, held)
     d_out[...] = d_hat
     join(1)
     rho1 = jnp.sqrt(alpha0 * alpha0 + beta1 * beta1)
@@ -491,10 +492,7 @@
     rhobar = -cosine * alpha1
     phi1 = cosine * beta0
     phibar = sine * beta0
-    total = row_send[...]
-    arrived(row_recv.at[pl.ds(1, chips - 1)], recv.at[5])
-    for q in range(1, chips):
-        total = total + row_recv[q]
+    total = row_sum(2)
     last_send[...] = total
     for m in range(1, 2 * nz):
         copy_last(m).start()
@@ -523,7 +521,7 @@
     has_left(x_send, send.at[2])
     has_left(y_send.at[:, others], send.at[3])
     has_left(pair_send, send.at[4])
-    has_left(row_recv.at[others], send.at[5])
+    has_left(row_recv.at[:, others], send.at[5])
     has_left(zrow_recv.at[:, zs], send.at[6])
     has_left(z_send.at[:, zs], send.at[7])
     has_left(v_full.at[:, zs], send.at[8])
@@ -608,8 +606,8 @@
             pltpu.VMEM((2, chips, rows, LANES), BF16),
             pltpu.VMEM((2, chips, rows, LANES), BF16),
             pltpu.VMEM((chips, rows, LANES), F32),
-            pltpu.VMEM((2, chips, rows + 16, LANES), BF16),
-            pltpu.VMEM((2, chips, rows + 16, LANES), BF16),
+            pltpu.VMEM((2, chips, rows, LANES), BF16),
+            pltpu.VMEM((2, chips, rows, LANES), BF16),
             pltpu.VMEM((tile_cols, rows, tile_size), F32),
             pltpu.VMEM((2, nz, *seg), BF16),
             pltpu.VMEM((2, nz, *seg), BF16),
@@ -622,14 +620,14 @@
             pltpu.VMEM((4, rows, LANES), F32),
             pltpu.VMEM((2, 1, LANES), F32),
             pltpu.VMEM((2, 1, LANES), F32),
-            pltpu.VMEM((1, LANES), F32),
-            pltpu.VMEM((chips, 1, LANES), F32),
+            pltpu.VMEM((3, 1, LANES), F32),
+            pltpu.VMEM((3, chips, 1, LANES), F32),
             pltpu.VMEM((2, 1, LANES), F32),
             pltpu.VMEM((2, nz, 1, LANES), F32),
             pltpu.VMEM((1, LANES), F32),
             pltpu.VMEM((2 * nz, 1, LANES), F32),
             dma((chips,)),
-            dma((14,)), dma((13,)),
+            dma((14,)), dma((14,)),
             dma((chips,)), dma((chips,)), dma((chips,)),
             dma((tile_cols,)), dma((tile_cols,)),
             dma((2,)), dma((2,)),

time: 83.4 us -> 82.3 us (0.987)
  Pallas kernels: 81.8 us -> 80.8 us
    pallas_call x1, Pallas kernels: 80 us -> 78.9 us  [on_device(): pl.pallas_call(functools.partial(kernel, dims), out_shape=[jax.ShapeDtype...]
where the time goes in v5:
time: 82.3 us; the launch traced here: 81.4 us
  Pallas kernels  80.8 us (98%)
    pallas_call x1, Pallas kernels, on_device(): pl.pallas_call(functools.partial(kernel, dims), out_shape=[jax.ShapeDtype...  78.9 us
    pallas_call x1, Pallas kernels, on_device(): pl.pallas_call(functools.partial(combine, nz), out_shape=[jax.ShapeDtypeS...  1.83 us

profile of v5, /device:TPU:0, one launch (start us, length us, event | category | flops | bytes accessed | tf_op | source)
XLA Modules:
  0.0 81.4 jit_solution(6620304511223551540)
XLA Ops:
  0.6 78.9 %lsqr.1 = (bf16[2,4,5,16,256]{4,3,2,1,0:T(8,128)(2,1)}, f32[8,128]{1,0:T(8,128)}, f32[64,128]{1,0:T(8,128)}, f32[2,5,16,256]{3,2,1,0:T(8,128)}) custom-call(f32[64,128]{1,0:T(8,128)} %bitcast.4, bf16[16,5,2,256,128]{4,3,2,1,0:T(8,128)(2,1)} %u_hbm.1, bf16[16,5,2,256,128]{4,3,2,1,0:T(8,128)(2,1)} %v_hbm.1, s32[5,16]{1,0:T(8,128)} %bitcast.5, s32[160]{0:T(256)} %assign.1), custom_call_target="tpu_custom_call" | custom-call | tf_op jit(solution)/shard_map/lsqr/pallas_call | solution.py:589
  79.6 1.8 %combine.1 = (f32[64,1280]{1,0:T(8,128)}, f32[1,32]{1,0:T(1,128)}) custom-call(f32[8,128]{1,0:T(8,128)} %get-tuple-element.6.scalars, bf16[2,4,5,16,256]{4,3,2,1,0:T(8,128)(2,1)} %get-tuple-element.7.natural), custom_call_target="tpu_custom_call" | custom-call | tf_op jit(solution)/shard_map/combine/pallas_call | solution.py:641
